TPU v7x, 256 devices: a whole 4x4x8 slice. The times are simulated.
256 devices in a mesh: space: 32 (over x_hi, z, core), tensor: 8 (over y, x_lo).
Axes of the slice: x: 4 (x_hi: 2, x_lo: 2; x = x_hi * 2 + x_lo), y: 4, z: 8, core: 2. Of those that a mesh axis runs over, the one named last changes fastest.
Arguments:
- field: bfloat16 [32, 32, 8192], P('space', None, 'tensor'), may hold values from -6 to 6
- w_in: bfloat16 [8192, 28672], P('tensor', 'space'), may hold values from -0.0625 to 0.0625
- w_out: bfloat16 [28672, 8192], P('space', 'tensor'), may hold values from -0.03125 to 0.03125
- kernel: float32 [9, 8192], P(None, 'tensor'), may hold values from -1.5 to 1.5
- cotangent: bfloat16 [32, 32, 8192], P('space', None, 'tensor'), may hold values from -6 to 6
Outputs:
- result: float32 [32, 32, 8192], P('space', None, 'tensor')
- field_grad: float32 [32, 32, 8192], P('space', None, 'tensor')
- grad_in: float32 [8192, 28672], P('tensor', 'space')
- grad_out: float32 [28672, 8192], P('space', 'tensor')
- grad_kernel: float32 [9, 8192], P(None, 'tensor')
All inputs are finite; a program needn't handle non-finite values.
Results may differ from a plain program's by a relative error of at most 0.029.
Values may be sent and summed in bfloat16 or wider, within the bound.
A program may use at most 128 MiB of HBM per device.

v0:
```python
import math

import jax
import jax.numpy as jnp
from jax import lax
from jax.sharding import PartitionSpec as P

OFFSETS = [(-1, -1), (-1, 0), (-1, 1), (0, -1), (0, 0), (0, 1), (1, -1), (1, 0), (1, 1)]


def extended(value, sides, width):
    for axis, dim in sides:
        size, length = (lax.axis_size(axis), value.shape[dim])
        up = [(i, (i + 1) % size) for i in range(size)]
        down = [(j, i) for i, j in up]
        last = lax.slice_in_dim(value, length - width, length, axis=dim)
        leading = lax.slice_in_dim(value, 0, width, axis=dim)
        before = lax.ppermute(last, axis, up)
        after = lax.ppermute(leading, axis, down)
        value = jnp.concatenate([before, value, after], axis=dim)
    return value


def spread_taps(padded, taps, own_rows):
    total = jnp.zeros((own_rows,) + padded.shape[1:], jnp.float32)
    for tap_index, (row_step, col_step) in enumerate(OFFSETS):
        window = padded[1 + row_step : 1 + row_step + own_rows].astype(jnp.float32)
        total = total + taps[tap_index] * jnp.roll(window, -col_step, axis=1)
    return total


def collect_taps(padded, taps, own_rows):
    total = jnp.zeros((own_rows,) + padded.shape[1:], jnp.float32)
    for tap_index, (row_step, col_step) in enumerate(OFFSETS):
        window = padded[1 - row_step : 1 - row_step + own_rows]
        total = total + taps[tap_index] * jnp.roll(window, col_step, axis=1)
    return total


def on_device(field, w_in, w_out, kernel, cotangent):
    own_rows = field.shape[0]
    factor = 1.0 / math.sqrt(own_rows * lax.axis_size("space") * field.shape[1])
    padded = extended(field, (("space", 0),), 1)
    mixed = (field.astype(jnp.float32) + spread_taps(padded, kernel, own_rows)).astype(jnp.bfloat16)
    gathered = lax.all_gather(mixed, "space", axis=0, tiled=True)
    rows_part = gathered
    hidden = lax.psum_scatter(
        jnp.einsum("rcd,df->rcf", rows_part, w_in, preferred_element_type=jnp.float32).astype(
            jnp.bfloat16
        ),
        "tensor",
        scatter_dimension=0,
        tiled=True,
    ).astype(jnp.float32)
    activ, gelu_back = jax.vjp(jax.nn.gelu, hidden)
    activation = activ.astype(jnp.bfloat16)
    acts_all = lax.all_gather(activation, "tensor", axis=0, tiled=True)
    rows_part = acts_all
    result = lax.psum_scatter(
        jnp.einsum("rcf,fd->rcd", rows_part, w_out, preferred_element_type=jnp.float32).astype(
            jnp.bfloat16
        ),
        "space",
        scatter_dimension=0,
        tiled=True,
    ).astype(jnp.float32)
    grads_all = lax.all_gather(cotangent, "space", axis=0, tiled=True)
    grad_out = (
        jnp.einsum("rcf,rcd->fd", acts_all, grads_all, preferred_element_type=jnp.float32) * factor
    )
    rows_part = grads_all
    act_grad = lax.psum_scatter(
        jnp.einsum("rcd,fd->rcf", rows_part, w_out, preferred_element_type=jnp.float32).astype(
            jnp.bfloat16
        ),
        "tensor",
        scatter_dimension=0,
        tiled=True,
    ).astype(jnp.float32)
    hidden_grad = gelu_back(act_grad)[0].astype(jnp.bfloat16)
    hidden_all = lax.all_gather(hidden_grad, "tensor", axis=0, tiled=True)
    grad_in = (
        jnp.einsum("rcd,rcf->df", gathered, hidden_all, preferred_element_type=jnp.float32) * factor
    )
    rows_part = hidden_all
    mixed_grad = lax.psum_scatter(
        jnp.einsum("rcf,df->rcd", rows_part, w_in, preferred_element_type=jnp.float32).astype(
            jnp.bfloat16
        ),
        "space",
        scatter_dimension=0,
        tiled=True,
    ).astype(jnp.float32)
    grad_padded = extended(mixed_grad, (("space", 0),), 1)
    field_grad = mixed_grad + collect_taps(grad_padded, kernel, own_rows)
    kernel_rows = []
    for tap_index, (row_step, col_step) in enumerate(OFFSETS):
        window = padded[1 + row_step : 1 + row_step + own_rows].astype(jnp.float32)
        moved = jnp.roll(window, -col_step, axis=1)
        kernel_rows.append(jnp.sum(mixed_grad * moved, axis=(0, 1)))
    grad_kernel = lax.psum(jnp.stack(kernel_rows, axis=0), "space") * factor
    return (result, field_grad, grad_in, grad_out, grad_kernel)


def solution(mesh):
    return jax.shard_map(
        on_device,
        mesh=mesh,
        in_specs=(
            P("space", None, "tensor"),
            P("tensor", "space"),
            P("space", "tensor"),
            P(None, "tensor"),
            P("space", None, "tensor"),
        ),
        out_specs=(
            P("space", None, "tensor"),
            P("space", None, "tensor"),
            P("tensor", "space"),
            P("space", "tensor"),
            P(None, "tensor"),
        ),
        check_vma=False,
    )
```

profile of v0, /device:TPU:1, one launch (start us, length us, event | category | flops | bytes accessed | tf_op | source)
XLA Modules:
  0.0 643.3 jit_solution(2380335795210704250)
XLA Ops:
  7.2 0.0 copy-start
  7.2 0.0 copy-start.2
  7.2 0.0 all-gather.9.cloned.1.call-start
  7.2 0.7 all-gather.9.cloned.1.call-update
  7.9 0.0 all-gather.5.cloned.1.call-start
  8.0 3.1 collective-permute-start
  11.1 0.3 collective-permute-start.1
  11.4 1.1 fusion.46
  12.5 0.9 fusion.50
  13.4 0.7 fusion.49
  14.2 0.0 collective-permute-done
  14.2 0.8 collective-permute-done.1
  15.0 0.0 copy-done.2
  15.1 0.8 add_convert_fusion
  15.9 0.0 all-gather.5.cloned.1.call-update
  15.9 0.0 reduce-scatter.9.cloned.1.call-start
  15.9 79.0 %all-gather.9.cloned.1.call-done = bf16[32,32,1024]{2,1,0:T(8,128)(2,1)} async-done(((bf16[1,32,1024]{2,1,0:T(8,128)(2,1)}), bf16[32,32,1024]{2,1,0:T(8,128)(2,1)}) %all-gather.9.cloned.1.call-update) | async-done | bytes 2097168 | tf_op jit(solution)/shard_map/all_gather | solution.py:67
  95.0 5.7 fusion.9
  100.7 0.0 reduce-scatter.9.cloned.1.call-update
  100.7 0.0 reduce-scatter.5.cloned.1.call-start
  100.8 74.1 %all-gather.5.cloned.1.call-done = bf16[32,32,1024]{2,1,0:T(8,128)(2,1)} async-done(((bf16[1,32,1024]{2,1,0:T(8,128)(2,1)}), bf16[32,32,1024]{2,1,0:T(8,128)(2,1)}) %all-gather.5.cloned.1.call-update) | async-done | bytes 2097168 | tf_op jit(solution)/shard_map/all_gather | solution.py:45
  174.9 0.0 copy-done
  174.9 5.1 fusion.6
  180.1 0.0 reduce-scatter.5.cloned.1.call-update
  180.1 0.0 all-gather.11.cloned.1.call-start
  180.2 44.2 %reduce-scatter.9.cloned.1.call-done = bf16[4,32,896]{2,1,0:T(8,128)(2,1)} async-done(((bf16[32,32,896]{2,1,0:T(8,128)(2,1)}), bf16[4,32,896]{2,1,0:T(8,128)(2,1)}) %reduce-scatter.9.cloned.1.call-update) | async-done | bytes 229392 | tf_op jit(solution)/shard_map/reduce_scatter | solution.py:72
  224.3 52.4 %reduce-scatter.5.cloned.1.call-done = bf16[4,32,896]{2,1,0:T(8,128)(2,1)} async-done(((bf16[32,32,896]{2,1,0:T(8,128)(2,1)}), bf16[4,32,896]{2,1,0:T(8,128)(2,1)}) %reduce-scatter.5.cloned.1.call-update) | async-done | bytes 229392 | tf_op jit(solution)/shard_map/reduce_scatter | solution.py:47
  276.7 2.2 fusion.15
  278.9 0.0 all-gather.11.cloned.1.call-update
  278.9 0.0 all-gather.7.cloned.1.call-start
  279.0 0.5 all-gather.7.cloned.1.call-update
  279.5 0.0 reduce-scatter.11.cloned.1.call-start
  279.6 48.5 %all-gather.11.cloned.1.call-done = bf16[32,32,896]{2,1,0:T(8,128)(2,1)} async-done(((bf16[4,32,896]{2,1,0:T(8,128)(2,1)}), bf16[32,32,896]{2,1,0:T(8,128)(2,1)}) %all-gather.11.cloned.1.call-update) | async-done | bytes 1835024 | tf_op jit(solution)/shard_map/all_gather | solution.py:81
  328.1 5.2 convolution_convert_fusion
  333.3 0.0 reduce-scatter.11.cloned.1.call-update
  333.3 0.2 reduce-scatter.7.cloned.1.call-start
  333.6 45.8 %all-gather.7.cloned.1.call-done = bf16[32,32,896]{2,1,0:T(8,128)(2,1)} async-done(((bf16[4,32,896]{2,1,0:T(8,128)(2,1)}), bf16[32,32,896]{2,1,0:T(8,128)(2,1)}) %all-gather.7.cloned.1.call-update) | async-done | bytes 1835024 | tf_op jit(solution)/shard_map/all_gather | solution.py:57
  379.4 5.7 convolution_convert_fusion.1
  385.1 0.0 reduce-scatter.7.cloned.1.call-update
  385.1 0.0 copy-start.3
  385.1 0.0 copy-start.4
  385.1 6.5 %bitcast_multiply_fusion.1 = f32[1024,896]{1,0:T(8,128)} fusion(bf16[32,32,1024]{2,1,0:T(8,128)(2,1)} %all-gather.5.cloned.1.call-done, bf16[32,32,896]{2,1,0:T(8,128)(2,1)} %all-gather.11.cloned.1.call-done), kind=kOutput, calls=%fused_computation.1 | convolution fusion | flops 1879965696 | bytes 7602176 | tf_op jit(solution)/shard_map/rcd,rcf->df/dot_general | solution.py:83
  391.6 0.0 copy-done.3
  391.6 0.0 copy-done.4
  391.6 4.0 bitcast_multiply_fusion
  395.6 101.6 %reduce-scatter.11.cloned.1.call-done = bf16[1,32,1024]{2,1,0:T(8,128)(2,1)} async-done(((bf16[32,32,1024]{2,1,0:T(8,128)(2,1)}), bf16[1,32,1024]{2,1,0:T(8,128)(2,1)}) %reduce-scatter.11.cloned.1.call-update) | async-done | bytes 65552 | tf_op jit(solution)/shard_map/reduce_scatter | solution.py:86
  497.3 0.0 copy-start.1
  497.3 0.9 convert_element_type.71
  498.2 6.0 collective-permute-start.3
  504.2 0.0 collective-permute-start.2
  504.2 1.1 fusion.36
  505.2 0.1 stack.39
  505.3 128.0 %psum.7 = f32[9,1024]{1,0:T(8,128)S(1)} all-reduce(f32[9,1024]{1,0:T(8,128)S(1)} %stack.39), channel_id=1, replica_groups=mesh['space'=32,'tensor'=8] {'space'}, use_global_device_ids=true, to_apply=%region_13.14 | all-reduce | flops 9216 | bytes 73728 | tf_op jit(solution)/shard_map/psum | solution.py:101
  633.3 0.6 broadcast_multiply_fusion
  634.0 0.0 copy-done.1
  634.0 0.0 reduce-scatter.7.cloned.1.call-done
  634.0 1.5 convert_element_type.66
  635.5 0.0 collective-permute-done.3
  635.6 0.0 collective-permute-done.2
  635.6 0.8 convert_add_fusion.1
  (10 shorter events, 0.1 us)
Async XLA Ops:
  7.2 167.8 %copy-start = (bf16[1024,896]{1,0:T(8,128)(2,1)S(1)}, bf16[1024,896]{1,0:T(8,128)(2,1)}, u32[]{:S(2)}) copy-start(bf16[1024,896]{1,0:T(8,128)(2,1)} %param.6) | copy-start | bytes 5505028
  7.2 7.9 %copy-start.2 = (bf16[1,32,1024]{2,1,0:T(8,128)(2,1)S(1)}, bf16[1,32,1024]{2,1,0:T(8,128)(2,1)}, u32[]{:S(2)}) copy-start(bf16[1,32,1024]{2,1,0:T(8,128)(2,1)} %param.5) | copy-start | bytes 196612
  7.2 87.8 %all-gather.9.cloned.1.call-start = ((), (), s32[]{:S(2)}) async-start(), calls=%async_computation.8 | async-start | bytes 2162688 | tf_op jit(solution)/shard_map/all_gather | solution.py:67
  7.9 167.0 %all-gather.5.cloned.1.call-start = ((), (), s32[]{:S(2)}) async-start(), calls=%async_computation.4 | async-start | bytes 2162688 | tf_op jit(solution)/shard_map/all_gather | solution.py:45
  8.0 6.2 collective-permute-start
  11.1 3.9 collective-permute-start.1
  15.9 208.4 %reduce-scatter.9.cloned.1.call-start = ((), (), s32[]{:S(2)}) async-start(), calls=%async_computation.9 | async-start | bytes 2064384 | tf_op jit(solution)/shard_map/reduce_scatter | solution.py:72
  100.7 176.0 %reduce-scatter.5.cloned.1.call-start = ((), (), s32[]{:S(2)}) async-start(), calls=%async_computation.5 | async-start | bytes 2064384 | tf_op jit(solution)/shard_map/reduce_scatter | solution.py:47
  180.1 148.0 %all-gather.11.cloned.1.call-start = ((), (), s32[]{:S(2)}) async-start(), calls=%async_computation.10 | async-start | bytes 2064384 | tf_op jit(solution)/shard_map/all_gather | solution.py:81
  278.9 100.4 %all-gather.7.cloned.1.call-start = ((), (), s32[]{:S(2)}) async-start(), calls=%async_computation.6 | async-start | bytes 2064384 | tf_op jit(solution)/shard_map/all_gather | solution.py:57
  279.5 217.7 %reduce-scatter.11.cloned.1.call-start = ((), (), s32[]{:S(2)}) async-start(), calls=%async_computation.11 | async-start | bytes 2162688 | tf_op jit(solution)/shard_map/reduce_scatter | solution.py:86
  333.3 300.7 %reduce-scatter.7.cloned.1.call-start = ((), (), s32[]{:S(2)}) async-start(), calls=%async_computation.7 | async-start | bytes 2162688 | tf_op jit(solution)/shard_map/reduce_scatter | solution.py:59
  385.1 6.5 %copy-start.3 = (bf16[32,32,1024]{2,1,0:T(8,128)(2,1)S(1)}, bf16[32,32,1024]{2,1,0:T(8,128)(2,1)}, u32[]{:S(2)}) copy-start(bf16[32,32,1024]{2,1,0:T(8,128)(2,1)} %all-gather.9.cloned.1.call-done) | copy-start | bytes 6291460
  385.1 6.5 %copy-start.4 = (bf16[32,32,896]{2,1,0:T(8,128)(2,1)S(1)}, bf16[32,32,896]{2,1,0:T(8,128)(2,1)}, u32[]{:S(2)}) copy-start(bf16[32,32,896]{2,1,0:T(8,128)(2,1)} %all-gather.7.cloned.1.call-done) | copy-start | bytes 5505028
  497.3 136.7 %copy-start.1 = (bf16[1,32,1024]{2,1,0:T(8,128)(2,1)S(1)}, bf16[1,32,1024]{2,1,0:T(8,128)(2,1)}, u32[]{:S(2)}) copy-start(bf16[1,32,1024]{2,1,0:T(8,128)(2,1)} %reduce-scatter.11.cloned.1.call-done) | copy-start | bytes 196612
  498.2 137.3 %collective-permute-start.3 = (f32[1,32,1024]{2,1,0:T(8,128)S(1)}, f32[1,32,1024]{2,1,0:T(8,128)S(1)}, u32[]{:S(2)}, u32[]{:S(2)}) collective-permute-start(f32[1,32,1024]{2,1,0:T(8,128)S(1)} %convert_element_type.71), channel_id=1, source_target_pairs={{0,8},{8,16},{16,24},{24,32},{32,40},{40,48},{48,56},{56,64},{64,7... | collective-permute-start | bytes 393224 | tf_op jit(solution)/shard_map/ppermute | solution.py:18
  504.2 131.4 %collective-permute-start.2 = (f32[1,32,1024]{2,1,0:T(8,128)S(1)}, f32[1,32,1024]{2,1,0:T(8,128)S(1)}, u32[]{:S(2)}, u32[]{:S(2)}) collective-permute-start(f32[1,32,1024]{2,1,0:T(8,128)S(1)} %convert_element_type.71), channel_id=1, source_target_pairs={{8,0},{16,8},{24,16},{32,24},{40,32},{48,40},{56,48},{64,56},{72,6... | collective-permute-start | bytes 393224 | tf_op jit(solution)/shard_map/ppermute | solution.py:19
Sparse Core Ops, SparseCore 0:
  10.8 84.1 all-gather.8
  98.3 76.5 all-gather.4
  178.1 46.2 reduce-scatter.8
  227.3 49.3 reduce-scatter.4
  279.1 48.9 all-gather.10
  330.3 49.0 all-gather.6
  383.5 113.6 reduce-scatter.10
  502.0 117.7 reduce-scatter.6
where the time goes:
time: 648 us; the launch traced here: 643 us
  waiting for transfers between devices  448 us (69%)
  blocking collectives  128 us (20%)
  matrix products  32.2 us (5%)
  between operations  14.3 us (2%)
  starting transfers between devices  9.91 us (2%)
  other arithmetic  7.93 us (1%)
    psum x1, blocking collectives, on_device(): grad_kernel = lax.psum(jnp.stack(kernel_rows, axis=0), 'space') * factor  128 us
    reduce_scatter x1, waiting for transfers between devices, on_device(): lax.psum_scatter(jnp.einsum('rcf,df->rcd', rows_part, w_in, preferred_ele...  102 us
    all_gather x1, waiting for transfers between devices, on_device(): grads_all = lax.all_gather(cotangent, 'space', axis=0, tiled=True)  79 us
    all_gather x1, waiting for transfers between devices, on_device(): gathered = lax.all_gather(mixed, 'space', axis=0, tiled=True)  74.1 us
    reduce_scatter x1, waiting for transfers between devices, on_device(): lax.psum_scatter(jnp.einsum('rcd,df->rcf', rows_part, w_in, preferred_ele...  52.4 us
    all_gather x1, waiting for transfers between devices, on_device(): hidden_all = lax.all_gather(hidden_grad, 'tensor', axis=0, tiled=True)  48.5 us
    all_gather x1, waiting for transfers between devices, on_device(): acts_all = lax.all_gather(activation, 'tensor', axis=0, tiled=True)  45.8 us
    reduce_scatter x1, waiting for transfers between devices, on_device(): lax.psum_scatter(jnp.einsum('rcd,fd->rcf', rows_part, w_out, preferred_el...  44.2 us
  transfers between devices with their start and end apart: 12, of which 8 were waited for; matrix products, arithmetic and copies ran while one was open for 6% of the time, Pallas kernels for 0%

commit v1 on v0

v1 whole, which is shorter than its diff:
```python
import functools
import math

import jax
import jax.numpy as jnp
from jax import lax
from jax.experimental import pallas as pl
from jax.experimental.pallas import tpu as pltpu
from jax.sharding import PartitionSpec as P

MESH = pl.DeviceIdType.MESH
F32, BF16 = jnp.float32, jnp.bfloat16
OFFSETS = [(-1, -1), (-1, 0), (-1, 1), (0, -1), (0, 0), (0, 1), (1, -1), (1, 0), (1, 1)]

NZ, NY, NT = 8, 4, 8
COLS, TOKENS, DB, FB = 32, 1024, 1024, 896
FACTOR = 1.0 / math.sqrt(TOKENS)

ORDER = [0, 1, 7, 2, 6, 3, 5, 4]
POS = {dz: 128 * i for i, dz in enumerate(ORDER)}
CHUNKS = [(0, 128), (128, 256), (384, 256), (640, 256), (896, 128)]
CHUNK_DZ = [[0], [1, 7], [2, 6], [3, 5], [4]]
OWN = [0, 16, 48, 80, 112]
RELS = [(dy, dx) for dy in range(NY) for dx in range(2) if (dy, dx) != (0, 0)]


def gelu_pair(hidden):
    c = math.sqrt(2.0 / math.pi)
    square = hidden * hidden
    th = jnp.tanh(c * (hidden + 0.044715 * (square * hidden)))
    half = 0.5 * (1.0 + th)
    slope = half + 0.5 * hidden * (1.0 - th * th) * (c * (1.0 + (3.0 * 0.044715) * square))
    return hidden * half, slope


def kernel(
    field_ref, cot_ref, taps_ref, wi_hbm, wo_hbm,
    result_ref, fgrad_ref, kgrad_ref, a_hbm, hg_hbm, mx_hbm, ct_hbm,
    wi, wo, ct, mx, gp, hp, rg, rh, own_g, av, hv,
    pm, pr, sbm, sbr, qm, qr, rrm, rrr, xrm, xrr, halo, mg, mhalo,
    kp, kr, kz, kf, kg,
    lsem, halo_s, halo_r, ag_s, ag_r, sib_r, rs_s, rs_r, at_s, at_r,
    sc_s, sc_sib, sc_ring, sc_x, mh_s, mh_r, k_s, k_r,
):
    s, t = lax.axis_index("space"), lax.axis_index("tensor")
    core, z, xh = s % 2, (s // 2) % NZ, s // (2 * NZ)
    y, xl = t // 2, t % 2

    def zdev(dz):
        return ((xh * NZ + (z + dz) % NZ) * 2 + core, t)

    def tdev(rel):
        return (s, ((y + rel[0]) % NY) * 2 + (xl + rel[1]) % 2)

    xdev = (((1 - xh) * NZ + z) * 2 + core, t)
    sib = ((xh * NZ + z) * 2 + 1 - core, t)
    nxt, prv = ((s + 1) % 32, t), ((s + 31) % 32, t)

    def send(src, dst, ssem, rsem, dev):
        pltpu.make_async_remote_copy(
            src_ref=src, dst_ref=dst, send_sem=ssem, recv_sem=rsem, device_id=dev, device_id_type=MESH
        ).start()

    def await_bytes(ref, sem):
        pltpu.make_async_copy(ref, ref, sem).wait()

    load_wi = pltpu.make_async_copy(wi_hbm, wi, lsem.at[0])
    load_wo = pltpu.make_async_copy(wo_hbm, wo, lsem.at[1])
    load_wo.start()
    load_wi.start()

    partners = [tdev(r) for r in RELS] + [zdev(d) for d in range(1, NZ)] + [xdev, nxt, prv]
    barrier = pltpu.get_barrier_semaphore()
    for dev in partners:
        pl.semaphore_signal(barrier, inc=1, device_id=dev, device_id_type=MESH)
    ct[pl.ds(0, 32)] = cot_ref[...]
    halo[1] = field_ref[...]
    pl.semaphore_wait(barrier, len(partners))

    def ag_begin(buf, i):
        own = buf.at[pl.ds(0, 32)]
        send(own, buf.at[pl.ds(POS[7], 32)], ag_s.at[i], ag_r.at[i, 1], zdev(1))
        send(own, buf.at[pl.ds(POS[1], 32)], ag_s.at[i], ag_r.at[i, 2], zdev(-1))
        send(own, buf.at[pl.ds(32, 32)], ag_s.at[i], ag_r.at[i, 0], xdev)
        send(own, buf.at[pl.ds(64, 32)], ag_s.at[i], sib_r.at[i, 0], sib)

    def ag_cross(buf, i):
        got = buf.at[pl.ds(32, 32)]
        await_bytes(got, ag_r.at[i, 0])
        send(got, buf.at[pl.ds(POS[7] + 32, 32)], ag_s.at[i], ag_r.at[i, 3], zdev(1))
        send(got, buf.at[pl.ds(POS[1] + 32, 32)], ag_s.at[i], ag_r.at[i, 4], zdev(-1))
        send(got, buf.at[pl.ds(96, 32)], ag_s.at[i], sib_r.at[i, 0], sib)

    def ag_step(buf, i, j):
        for xr in range(2):
            for way, (dz, ahead, nz) in enumerate(((NZ - j, 1, NZ - j - 1), (j, -1, j + 1))):
                if j == 4 and way != xr:
                    continue
                piece = buf.at[pl.ds(POS[dz] + 32 * xr, 32)]
                await_bytes(piece, ag_r.at[i, 4 * (j - 1) + 1 + 2 * xr + way])
                if j < 3 or (j == 3 and way == xr):
                    send(
                        piece, buf.at[pl.ds(POS[nz] + 32 * xr, 32)], ag_s.at[i],
                        ag_r.at[i, 4 * j + 1 + 2 * xr + way], zdev(ahead),
                    )
        for dz in CHUNK_DZ[j]:
            send(buf.at[pl.ds(POS[dz], 64)], buf.at[pl.ds(POS[dz] + 64, 64)], ag_s.at[i], sib_r.at[i, dz], sib)

    def ag_ready(buf, i, j):
        for dz in CHUNK_DZ[j]:
            await_bytes(buf.at[pl.ds(POS[dz] + 64, 64)], sib_r.at[i, dz])

    def mm(src, w, out, chunk, width, transposed):
        first, length = CHUNKS[chunk]
        left = src.at[pl.ds(first, length)]

        def tile(i, carry):
            at = pl.multiple_of(jnp.minimum(i * 256, width - 256), 128)
            if transposed:
                block = lax.dot_general(
                    left[...], w[pl.ds(at, 256), :], (((1,), (1,)), ((), ())), preferred_element_type=F32
                )
            else:
                block = jnp.dot(left[...], w[:, pl.ds(at, 256)], preferred_element_type=F32)
            out[pl.ds(first, length), pl.ds(at, 256)] = block.astype(BF16)
            return carry

        lax.fori_loop(0, 4, tile, 0)

    def rs_send(part, recv, i, chunk):
        first, length = CHUNKS[chunk]
        w = length // NT
        for slot, rel in enumerate(RELS):
            dev = tdev(rel)
            src = part.at[pl.ds(pl.multiple_of(first + dev[1] * w, w), w)]
            send(src, recv.at[pl.ds(7 * OWN[chunk] + slot * w, w)], rs_s.at[i, chunk], rs_r.at[i, chunk], dev)

    def rs_sum(part, recv, i, chunk):
        first, length = CHUNKS[chunk]
        w = length // NT
        await_bytes(recv.at[pl.ds(7 * OWN[chunk], 7 * w)], rs_r.at[i, chunk])
        total = part[pl.ds(pl.multiple_of(first + t * w, w), w)].astype(F32)
        for slot in range(7):
            total = total + recv[pl.ds(7 * OWN[chunk] + slot * w, w)].astype(F32)
        return total

    def at_send(buf, i, chunk):
        first, length = CHUNKS[chunk]
        w = length // NT
        mine = buf.at[pl.ds(pl.multiple_of(first + t * w, w), w)]
        for rel in RELS:
            send(mine, mine, at_s.at[i, chunk], at_r.at[i, chunk], tdev(rel))

    def at_wait(buf, i, chunk):
        first, length = CHUNKS[chunk]
        await_bytes(buf.at[pl.ds(first, 7 * length // NT)], at_r.at[i, chunk])

    def sc_sibling(part, sb, i, chunk):
        for dz in CHUNK_DZ[chunk]:
            send(part.at[pl.ds(POS[dz] + 64, 64)], sb.at[pl.ds(64 * dz, 64)], sc_s.at[i], sc_sib.at[i, dz], sib)

    def sc_chunk(part, sb, q, rr, i, chunk):
        for dz in CHUNK_DZ[chunk]:
            await_bytes(sb.at[pl.ds(64 * dz, 64)], sc_sib.at[i, dz])
            total = part[pl.ds(POS[dz], 64)].astype(F32) + sb[pl.ds(64 * dz, 64)].astype(F32)
            here = q.at[pl.ds(64 * dz, 64)]
            if dz == 4:
                here[...] = total.astype(BF16)
                send(q.at[pl.ds(256, 32)], rr.at[pl.ds(64 * 3, 32)], sc_s.at[i], sc_ring.at[i, 3], zdev(1))
                send(q.at[pl.ds(288, 32)], rr.at[pl.ds(64 * 5 + 32, 32)], sc_s.at[i], sc_ring.at[i, 5], zdev(-1))
            elif dz in (3, 5):
                here[...] = total.astype(BF16)
                half = 0 if dz == 3 else 32
                more = rr.at[pl.ds(64 * dz + half, 32)]
                await_bytes(more, sc_ring.at[i, dz])
                rows = pl.ds(64 * dz + half, 32)
                q[rows] = (total[half : half + 32] + more[...].astype(F32)).astype(BF16)
            elif dz != 0:
                more = rr.at[pl.ds(64 * dz, 64)]
                await_bytes(more, sc_ring.at[i, dz])
                here[...] = (total + more[...].astype(F32)).astype(BF16)
            if dz in (1, 2, 3):
                to = 8 if dz == 1 else dz - 1
                send(here, rr.at[pl.ds(64 * to, 64)], sc_s.at[i], sc_ring.at[i, to], zdev(1))
            if dz in (5, 6, 7):
                to = 0 if dz == 7 else dz + 1
                send(here, rr.at[pl.ds(64 * to, 64)], sc_s.at[i], sc_ring.at[i, to], zdev(-1))
            if dz == 0:
                for slot in (8, 0):
                    more = rr.at[pl.ds(64 * slot, 64)]
                    await_bytes(more, sc_ring.at[i, slot])
                    total = total + more[...].astype(F32)
                q[pl.ds(32, 32)] = total[32:].astype(BF16)
                return total[:32]

    def sc_cross(q, xr, i):
        send(q.at[pl.ds(32, 32)], xr, sc_s.at[i], sc_x.at[i], xdev)

    send(field_ref, halo.at[0], halo_s.at[0], halo_r.at[0], nxt)
    send(field_ref, halo.at[2], halo_s.at[1], halo_r.at[1], prv)
    ag_begin(ct, 0)
    await_bytes(halo.at[0], halo_r.at[0])
    await_bytes(halo.at[2], halo_r.at[1])

    def conv_tile(i, carry):
        lanes = pl.ds(pl.multiple_of(i * 128, 128), 128)
        rows = [halo[r, :, lanes].astype(F32) for r in range(3)]
        total = jnp.zeros((COLS, 128), F32)
        for k, (dr, dc) in enumerate(OFFSETS):
            moved = rows[1 + dr] if dc == 0 else pltpu.roll(rows[1 + dr], (-dc) % COLS, 0)
            total = total + taps_ref[k : k + 1, lanes] * moved
        mx[pl.ds(0, 32), lanes] = (rows[1] + total).astype(BF16)
        return carry

    lax.fori_loop(0, 8, conv_tile, 0)
    ag_cross(ct, 0)
    ag_begin(mx, 1)
    load_wo.wait()

    for c in range(5):
        if c > 0:
            ag_step(ct, 0, c)
        if c == 1:
            ag_cross(mx, 1)
        if c > 1:
            ag_step(mx, 1, c - 1)
        ag_ready(ct, 0, c)
        mm(ct, wo, gp, c, FB, True)
        rs_send(gp, rg, 0, c)
    store_ct = pltpu.make_async_copy(ct, ct_hbm, lsem.at[2])
    store_ct.start()
    ag_step(mx, 1, 4)
    load_wi.wait()
    for c in range(5):
        ag_ready(mx, 1, c)
    store_mx = pltpu.make_async_copy(mx, mx_hbm, lsem.at[3])
    store_mx.start()
    for c in range(4, -1, -1):
        mm(mx, wi, hp, c, FB, False)
        rs_send(hp, rh, 1, c)
    for c in range(5):
        own_g[pl.ds(OWN[c], CHUNKS[c][1] // NT)] = rs_sum(gp, rg, 0, c)
    for c in range(4, -1, -1):
        first, length = CHUNKS[c]
        w = length // NT
        act, slope = gelu_pair(rs_sum(hp, rh, 1, c))
        rows = pl.ds(pl.multiple_of(first + t * w, w), w)
        hv[rows] = (own_g[pl.ds(OWN[c], w)] * slope).astype(BF16)
        av[rows] = act.astype(BF16)
        at_send(hv, 0, c)
    for c in range(4, -1, -1):
        at_send(av, 1, c)

    mgrow = None
    for c in range(4, -1, -1):
        at_wait(hv, 0, c)
        mm(hv, wi, pm, c, DB, True)
        sc_sibling(pm, sbm, 0, c)
        mgrow = sc_chunk(pm, sbm, qm, rrm, 0, c)
    sc_cross(qm, xrm, 0)
    mg[...] = mgrow
    store_hg = pltpu.make_async_copy(hv, hg_hbm, lsem.at[4])
    store_hg.start()

    def k_stage(i):
        if i == 0:
            await_bytes(xrm, sc_x.at[0])
            mg[...] = mg[...] + xrm[...].astype(F32)
            send(mg, mhalo.at[0], mh_s.at[0], mh_r.at[0], nxt)
            send(mg, mhalo.at[1], mh_s.at[1], mh_r.at[1], prv)

            def kgrad_tile(n, carry):
                lanes = pl.ds(pl.multiple_of(n * 128, 128), 128)
                grad = mg[:, lanes]
                rows = [halo[r, :, lanes].astype(F32) for r in range(3)]
                sums = []
                for dr, dc in OFFSETS:
                    moved = rows[1 + dr] if dc == 0 else pltpu.roll(rows[1 + dr], (-dc) % COLS, 0)
                    sums.append(jnp.sum(grad * moved, axis=0, keepdims=True))
                kp[n] = jnp.concatenate(sums + [jnp.zeros((7, 128), F32)], axis=0)
                return carry

            lax.fori_loop(0, 8, kgrad_tile, 0)
            send(kp, kr.at[0], k_s.at[0], k_r.at[0], sib)
        if i == 1:
            await_bytes(kr.at[0], k_r.at[0])
            await_bytes(kp, k_s.at[0])
            kp[...] = kp[...] + kr[0]
            send(kp, kr.at[1], k_s.at[1], k_r.at[1], xdev)
            await_bytes(mhalo.at[0], mh_r.at[0])
            await_bytes(mhalo.at[1], mh_r.at[1])

            def fgrad_tile(n, carry):
                lanes = pl.ds(pl.multiple_of(n * 128, 128), 128)
                rows = [mhalo[0, :, lanes], mg[:, lanes], mhalo[1, :, lanes]]
                total = rows[1]
                for k, (dr, dc) in enumerate(OFFSETS):
                    moved = rows[1 - dr] if dc == 0 else pltpu.roll(rows[1 - dr], dc % COLS, 0)
                    total = total + taps_ref[k : k + 1, lanes] * moved
                fgrad_ref[:, lanes] = total
                return carry

            lax.fori_loop(0, 8, fgrad_tile, 0)
        if i == 2:
            await_bytes(kr.at[1], k_r.at[1])
            await_bytes(kp, k_s.at[1])
            kp[...] = kp[...] + kr[1]
            for d in range(1, NZ):
                dev = zdev(d)
                send(kp.at[(z + d) % NZ], kz.at[d - 1], k_s.at[2], k_r.at[2], dev)
        if i == 3:
            await_bytes(kz, k_r.at[2])
            total = kp[z]
            for d in range(7):
                total = total + kz[d]
            kf[...] = total
            kg[z] = total
            for d in range(1, NZ):
                send(kf, kg.at[z], k_s.at[3], k_r.at[3], zdev(d))
        if i == 4:
            await_bytes(kg.at[pl.ds(0, 7)], k_r.at[3])
            for n in range(8):
                kgrad_ref[:, 128 * n : 128 * (n + 1)] = kg[n, 0:9] * FACTOR

    row = None
    for c in range(4, -1, -1):
        at_wait(av, 1, c)
        mm(av, wo, pr, c, DB, False)
        sc_sibling(pr, sbr, 1, c)
        if c < 4:
            k_stage(3 - c)
        row = sc_chunk(pr, sbr, qr, rrr, 1, c)
    sc_cross(qr, xrr, 1)
    store_a = pltpu.make_async_copy(av, a_hbm, lsem.at[5])
    store_a.start()
    result_ref[...] = row
    k_stage(4)
    await_bytes(xrr, sc_x.at[1])
    result_ref[...] = result_ref[...] + xrr[...].astype(F32)

    for cp in (store_ct, store_mx, store_hg, store_a):
        cp.wait()
    for i in range(2):
        await_bytes(halo.at[0], halo_s.at[i])
        await_bytes(mhalo.at[0], mh_s.at[i])
        await_bytes(ct.at[pl.ds(0, 992)], ag_s.at[i])
        for c in range(5):
            n = 7 * CHUNKS[c][1] // NT
            await_bytes(gp.at[pl.ds(0, n)], rs_s.at[i, c])
            await_bytes(hv.at[pl.ds(0, n)], at_s.at[i, c])
        await_bytes(pm.at[pl.ds(0, 992)], sc_s.at[i])
    await_bytes(kz, k_s.at[2])
    await_bytes(kz, k_s.at[3])


def on_device(field, w_in, w_out, taps, cotangent):
    vm, hbm = pl.BlockSpec(memory_space=pltpu.VMEM), pl.BlockSpec(memory_space=pl.ANY)
    dma = pltpu.SemaphoreType.DMA
    shapes = [
        ((COLS, DB), F32), ((COLS, DB), F32), ((9, DB), F32),
        ((TOKENS, FB), BF16), ((TOKENS, FB), BF16), ((TOKENS, DB), BF16), ((TOKENS, DB), BF16),
    ]
    scratch = [
        pltpu.VMEM((DB, FB), BF16), pltpu.VMEM((FB, DB), BF16),
        pltpu.VMEM((TOKENS, DB), BF16), pltpu.VMEM((TOKENS, DB), BF16),
        pltpu.VMEM((TOKENS, FB), BF16), pltpu.VMEM((TOKENS, FB), BF16),
        pltpu.VMEM((7 * 128, FB), BF16), pltpu.VMEM((7 * 128, FB), BF16),
        pltpu.VMEM((128, FB), F32),
        pltpu.VMEM((TOKENS, FB), BF16), pltpu.VMEM((TOKENS, FB), BF16),
        pltpu.VMEM((TOKENS, DB), BF16), pltpu.VMEM((TOKENS, DB), BF16),
        pltpu.VMEM((512, DB), BF16), pltpu.VMEM((512, DB), BF16),
        pltpu.VMEM((512, DB), BF16), pltpu.VMEM((512, DB), BF16),
        pltpu.VMEM((576, DB), BF16), pltpu.VMEM((576, DB), BF16),
        pltpu.VMEM((32, DB), BF16), pltpu.VMEM((32, DB), BF16),
        pltpu.VMEM((3, COLS, DB), BF16), pltpu.VMEM((COLS, DB), F32), pltpu.VMEM((2, COLS, DB), F32),
        pltpu.VMEM((8, 16, 128), F32), pltpu.VMEM((2, 8, 16, 128), F32), pltpu.VMEM((7, 16, 128), F32),
        pltpu.VMEM((16, 128), F32), pltpu.VMEM((8, 16, 128), F32),
        dma((6,)), dma((2,)), dma((2,)), dma((2,)), dma((2, 17)), dma((2, 8)),
        dma((2, 5)), dma((2, 5)), dma((2, 5)), dma((2, 5)),
        dma((2,)), dma((2, 8)), dma((2, 9)), dma((2,)), dma((2,)), dma((2,)), dma((4,)), dma((4,)),
    ]
    result, fgrad, kgrad, acts, hgrads, mixed, cots = pl.pallas_call(
        kernel,
        out_shape=[jax.ShapeDtypeStruct(*x) for x in shapes],
        in_specs=[vm, vm, vm, hbm, hbm],
        out_specs=[vm, vm, vm, hbm, hbm, hbm, hbm],
        scratch_shapes=scratch,
        compiler_params=pltpu.CompilerParams(
            collective_id=0, has_side_effects=True, vmem_limit_bytes=60 * 2**20
        ),
        cost_estimate=pl.CostEstimate(flops=4 * 2 * 1024 * 1024 * 896, bytes_accessed=12 * 2**20, transcendentals=0),
        name="block",
    )(field.reshape(COLS, DB), cotangent.reshape(COLS, DB), taps, w_in, w_out)
    grad_out = jnp.einsum("tf,td->fd", acts, cots, preferred_element_type=F32) * FACTOR
    grad_in = jnp.einsum("td,tf->df", mixed, hgrads, preferred_element_type=F32) * FACTOR
    return (result.reshape(1, COLS, DB), fgrad.reshape(1, COLS, DB), grad_in, grad_out, kgrad)


def solution(mesh):
    space = P("space", None, "tensor")
    return jax.shard_map(
        on_device,
        mesh=mesh,
        in_specs=(space, P("tensor", "space"), P("space", "tensor"), P(None, "tensor"), space),
        out_specs=(space, space, P("tensor", "space"), P("space", "tensor"), P(None, "tensor")),
        check_vma=False,
    )
```

time: 648 us -> 140 us (0.22)
  waiting for transfers between devices: 448 us -> 0 us
  blocking collectives: 128 us -> 0 us
  Pallas kernels: 0 us -> 126 us
  matrix products: 32.2 us -> 10.5 us
  between operations: 14.3 us -> 0.68 us
  starting transfers between devices: 9.91 us -> 0 us
  other arithmetic: 7.93 us -> 0 us
    all_gather x4 -> x0, waiting for transfers between devices: 248 us -> none  [the longest x1 79 us: on_device(): grads_all = lax.all_gather(cotangent, 'space', axis=0, tiled=True)]
    reduce_scatter x4 -> x0, waiting for transfers between devices: 198 us -> none  [the longest x1 102 us: on_device(): lax.psum_scatter(jnp.einsum('rcf,df->rcd', rows_part, w_in, preferred_ele...]
    psum x1 -> x0, blocking collectives: 128 us -> none  [on_device(): grad_kernel = lax.psum(jnp.stack(kernel_rows, axis=0), 'space') * factor]
    pallas_call x0 -> x1, Pallas kernels: none -> 126 us  [on_device(): pl.pallas_call(kernel, out_shape=[jax.ShapeDtypeStruct(*x) for x in shape...]
    dot_general x6 -> x2, matrix products: 32.2 us -> 10.5 us  [the longest x1 6.5 us: on_device(): jnp.einsum('td,tf->df', mixed, hgrads, preferred_element_type=F32) * FACTOR]
    ppermute x4 -> x0, starting transfers between devices: 9.41 us -> none  [the longest x2 9.1 us: extended(): before = lax.ppermute(last, axis, up)]
  transfers between devices with their start and end apart: 12 -> 0, of which waited for: 8 -> 0; matrix products, arithmetic and copies ran while one was open for 6% -> 0% of each run, Pallas kernels for 0% -> 0%
where the time goes in v1:
time: 140 us; the launch traced here: 139 us
  Pallas kernels  126 us (90%)
  matrix products  10.5 us (8%)
  local copies, waits for them, and re-layouts  1.96 us (1%)
    pallas_call x1, Pallas kernels, on_device(): pl.pallas_call(kernel, out_shape=[jax.ShapeDtypeStruct(*x) for x in shape...  126 us
    dot_general x1, matrix products, on_device(): jnp.einsum('td,tf->df', mixed, hgrads, preferred_element_type=F32) * FACTOR  6.5 us
    dot_general x1, matrix products, on_device(): jnp.einsum('tf,td->fd', acts, cots, preferred_element_type=F32) * FACTOR  3.97 us

profile of v1, /device:TPU:1, one launch (start us, length us, event | category | flops | bytes accessed | tf_op | source)
XLA Modules:
  0.0 139.3 jit_solution(10560167912049222829)
XLA Ops:
  0.6 126.2 %block.1 = (f32[32,1024]{1,0:T(8,128)}, f32[32,1024]{1,0:T(8,128)}, f32[9,1024]{1,0:T(8,128)}, bf16[1024,896]{1,0:T(8,128)(2,1)}, bf16[1024,896]{1,0:T(8,128)(2,...) custom-call(bf16[32,1024]{1,0:T(8,128)(2,1)} %bitcast.10, bf16[32,1024]{1,0:T(8,128)(2,1)} %bitcast.11, ...), custom_call_target="tpu_custom_call" | custom-call | flops 7516192768 | bytes 12582912 | tf_op jit(solution)/shard_map/block/pallas_call | solution.py:382
  126.8 0.0 copy-start.3
  126.8 0.0 copy-start.4
  126.8 6.5 %convolution_multiply_fusion.1 = f32[1024,896]{1,0:T(8,128)} fusion(bf16[1024,1024]{1,0:T(8,128)(2,1)} %get-tuple-element.14, bf16[1024,896]{1,0:T(8,128)(2,1)} %get-tuple-element.15), kind=kOutput, calls=%fused_computation.1 | convolution fusion | flops 1879965696 | bytes 7602176 | tf_op jit(solution)/shard_map/td,tf->df/dot_general | solution.py:395
  133.3 0.0 copy-done.3
  133.3 0.0 copy-done.4
  133.3 0.0 copy-start.1
  133.3 0.0 copy-start
  133.4 0.0 copy-start.2
  133.4 4.0 %convolution_multiply_fusion = f32[896,1024]{1,0:T(8,128)} fusion(bf16[1024,896]{1,0:T(8,128)(2,1)S(1)} %copy-done.4, bf16[1024,1024]{1,0:T(8,128)(2,1)S(1)} %copy-done.3), kind=kOutput, calls=%fused_computation | convolution fusion | flops 1879965696 | bytes 7602176 | tf_op jit(solution)/shard_map/tf,td->fd/dot_general | solution.py:394
  137.3 0.0 copy-done.1
  137.3 0.7 copy.13
  138.0 0.0 copy-done
  138.0 0.7 copy.14
  138.6 0.0 copy-done.2
  138.7 0.6 copy.15
Async XLA Ops:
  126.8 6.5 %copy-start.3 = (bf16[1024,1024]{1,0:T(8,128)(2,1)S(1)}, bf16[1024,1024]{1,0:T(8,128)(2,1)}, u32[]{:S(2)}) copy-start(bf16[1024,1024]{1,0:T(8,128)(2,1)} %get-tuple-element.17) | copy-start | bytes 6291460
  126.8 6.5 %copy-start.4 = (bf16[1024,896]{1,0:T(8,128)(2,1)S(1)}, bf16[1024,896]{1,0:T(8,128)(2,1)}, u32[]{:S(2)}) copy-start(bf16[1024,896]{1,0:T(8,128)(2,1)} %get-tuple-element.16) | copy-start | bytes 5505028
  133.3 4.0 %copy-start.1 = (f32[32,1024]{1,0:T(8,128)S(1)}, f32[32,1024]{1,0:T(8,128)}, u32[]{:S(2)}) copy-start(f32[32,1024]{1,0:T(8,128)} %get-tuple-element.12) | copy-start | bytes 393220
  133.3 4.6 %copy-start = (f32[32,1024]{1,0:T(8,128)S(1)}, f32[32,1024]{1,0:T(8,128)}, u32[]{:S(2)}) copy-start(f32[32,1024]{1,0:T(8,128)} %get-tuple-element.13) | copy-start | bytes 393220
  133.4 5.3 %copy-start.2 = (f32[9,1024]{1,0:T(8,128)S(1)}, f32[9,1024]{1,0:T(8,128)}, u32[]{:S(2)}) copy-start(f32[9,1024]{1,0:T(8,128)} %get-tuple-element.28) | copy-start | bytes 110596

commit v2 on v1

v2 whole, which is shorter than its diff:
```python
import functools
import math

import jax
import jax.numpy as jnp
from jax import lax
from jax.experimental import pallas as pl
from jax.experimental.pallas import tpu as pltpu
from jax.sharding import PartitionSpec as P

MESH = pl.DeviceIdType.MESH
F32, BF16 = jnp.float32, jnp.bfloat16
OFFSETS = [(-1, -1), (-1, 0), (-1, 1), (0, -1), (0, 0), (0, 1), (1, -1), (1, 0), (1, 1)]

NZ, NY, NT = 8, 4, 8
COLS, TOKENS, DB, FB = 32, 1024, 1024, 896
FACTOR = 1.0 / math.sqrt(TOKENS)

ORDER = [0, 1, 7, 2, 6, 3, 5, 4]
POS = {dz: 128 * i for i, dz in enumerate(ORDER)}
CHUNKS = [(0, 128), (128, 256), (384, 256), (640, 256), (896, 128)]
CHUNK_DZ = [[0], [1, 7], [2, 6], [3, 5], [4]]
OWN = [0, 16, 48, 80, 112]
CA = 512
CB = FB - CA
PA, PB = pl.ds(0, CA), pl.ds(CA, CB)


def gelu_pair(hidden):
    c = math.sqrt(2.0 / math.pi)
    square = hidden * hidden
    th = jnp.tanh(c * (hidden + 0.044715 * (square * hidden)))
    half = 0.5 * (1.0 + th)
    slope = half + 0.5 * hidden * (1.0 - th * th) * (c * (1.0 + (3.0 * 0.044715) * square))
    return hidden * half, slope


def kernel(
    field_ref, cot_ref, taps_ref, wi_hbm, wo_hbm,
    result_ref, fgrad_ref, kgrad_ref, gin, gout,
    wi, wo, ct, mx, gp, hp, xa, ya, yain, ybin, xb, xbin, ownb, av, hv,
    pm, pr, sbm, sbr, qm, qr, rrm, rrr, finm, finr, halo, mg, mhalo,
    kp, kr, kz, kf, kg,
    lsem, halo_s, halo_r, ag_s, ag_r, sib_r, rs_s, rs_r, at_s, at_r,
    sc_s, sc_sib, sc_ring, sc_fin, mh_s, mh_r, k_s, k_r,
):
    s, t = lax.axis_index("space"), lax.axis_index("tensor")
    core, z, xh = s % 2, (s // 2) % NZ, s // (2 * NZ)
    y, xl = t // 2, t % 2

    def zdev(dz):
        return ((xh * NZ + (z + dz) % NZ) * 2 + core, t)

    def ydev(dy):
        return (s, ((y + dy) % NY) * 2 + xl)

    def zxdev(dz):
        return (((1 - xh) * NZ + (z + dz) % NZ) * 2 + core, t)

    xdev = (((1 - xh) * NZ + z) * 2 + core, t)
    ldev = (s, y * 2 + 1 - xl)
    sib = ((xh * NZ + z) * 2 + 1 - core, t)
    nxt, prv = ((s + 1) % 32, t), ((s + 31) % 32, t)

    def send(src, dst, ssem, rsem, dev):
        pltpu.make_async_remote_copy(
            src_ref=src, dst_ref=dst, send_sem=ssem, recv_sem=rsem, device_id=dev, device_id_type=MESH
        ).start()

    def await_bytes(ref, sem):
        pltpu.make_async_copy(ref, ref, sem).wait()

    load_wi = pltpu.make_async_copy(wi_hbm, wi, lsem.at[0])
    load_wo = pltpu.make_async_copy(wo_hbm, wo, lsem.at[1])
    load_wo.start()
    load_wi.start()

    partners = [ydev(d) for d in range(1, NY)] + [zdev(d) for d in range(1, NZ)]
    partners += [zxdev(d) for d in range(NZ)] + [ldev, nxt, prv]
    barrier = pltpu.get_barrier_semaphore()
    for dev in partners:
        pl.semaphore_signal(barrier, inc=1, device_id=dev, device_id_type=MESH)
    ct[pl.ds(0, 32)] = cot_ref[...]
    halo[1] = field_ref[...]
    pl.semaphore_wait(barrier, len(partners))

    def ag_begin(buf, i):
        own = buf.at[pl.ds(0, 32)]
        send(own, buf.at[pl.ds(POS[7], 32)], ag_s.at[i], ag_r.at[i, 1], zdev(1))
        send(own, buf.at[pl.ds(POS[1], 32)], ag_s.at[i], ag_r.at[i, 2], zdev(-1))
        send(own, buf.at[pl.ds(32, 32)], ag_s.at[i], ag_r.at[i, 0], xdev)
        send(own, buf.at[pl.ds(64, 32)], ag_s.at[i], sib_r.at[i, 0], sib)

    def ag_cross(buf, i):
        got = buf.at[pl.ds(32, 32)]
        await_bytes(got, ag_r.at[i, 0])
        send(got, buf.at[pl.ds(POS[7] + 32, 32)], ag_s.at[i], ag_r.at[i, 3], zdev(1))
        send(got, buf.at[pl.ds(POS[1] + 32, 32)], ag_s.at[i], ag_r.at[i, 4], zdev(-1))
        send(got, buf.at[pl.ds(96, 32)], ag_s.at[i], sib_r.at[i, 0], sib)

    def ag_step(buf, i, j):
        for xr in range(2):
            for way, (dz, ahead, nz) in enumerate(((NZ - j, 1, NZ - j - 1), (j, -1, j + 1))):
                if j == 4 and way != xr:
                    continue
                piece = buf.at[pl.ds(POS[dz] + 32 * xr, 32)]
                await_bytes(piece, ag_r.at[i, 4 * (j - 1) + 1 + 2 * xr + way])
                if j < 3 or (j == 3 and way == xr):
                    send(
                        piece, buf.at[pl.ds(POS[nz] + 32 * xr, 32)], ag_s.at[i],
                        ag_r.at[i, 4 * j + 1 + 2 * xr + way], zdev(ahead),
                    )
        for dz in CHUNK_DZ[j]:
            send(buf.at[pl.ds(POS[dz], 64)], buf.at[pl.ds(POS[dz] + 64, 64)], ag_s.at[i], sib_r.at[i, dz], sib)

    def ag_ready(buf, i, j):
        for dz in CHUNK_DZ[j]:
            await_bytes(buf.at[pl.ds(POS[dz] + 64, 64)], sib_r.at[i, dz])

    def mm(src, w, out, chunk, transposed):
        first, length = CHUNKS[chunk]
        left = src.at[pl.ds(first, length)]

        if transposed:
            block = lax.dot_general(left[...], w[...], (((1,), (1,)), ((), ())), preferred_element_type=F32)
        else:
            block = jnp.dot(left[...], w[...], preferred_element_type=F32)
        out[pl.ds(first, length)] = block.astype(BF16)

    def rows_of(start, length, w):
        return pl.ds(pl.multiple_of(start, w), length)

    def rs_first(part, i, c):
        first, w = CHUNKS[c][0], CHUNKS[c][1] // NT
        send(
            part.at[rows_of(first + (1 - xl) * 4 * w, 4 * w, w), PA], xa.at[i, pl.ds(4 * OWN[c], 4 * w)],
            rs_s.at[i, c], rs_r.at[i, c, 0], ldev,
        )
        for d in range(1, NY):
            to = (y + d) % NY
            send(
                part.at[rows_of(first + to * 2 * w, 2 * w, w), PB],
                ybin.at[i, pl.ds(6 * OWN[c] + (d - 1) * 2 * w, 2 * w)],
                rs_s.at[i, c], rs_r.at[i, c, 1], ydev(d),
            )

    def rs_second(part, i, c):
        first, w = CHUNKS[c][0], CHUNKS[c][1] // NT
        got = xa.at[i, pl.ds(4 * OWN[c], 4 * w)]
        await_bytes(got, rs_r.at[i, c, 0])
        mine = part[rows_of(first + xl * 4 * w, 4 * w, w), PA].astype(F32)
        ya[i, pl.ds(4 * OWN[c], 4 * w)] = (mine + got[...].astype(F32)).astype(BF16)
        for d in range(1, NY):
            to = (y + d) % NY
            send(
                ya.at[i, rows_of(4 * OWN[c] + to * w, w, w)], yain.at[i, pl.ds(3 * OWN[c] + (d - 1) * w, w)],
                rs_s.at[i, c], rs_r.at[i, c, 2], ydev(d),
            )
        await_bytes(ybin.at[i, pl.ds(6 * OWN[c], 6 * w)], rs_r.at[i, c, 1])
        for own in range(2):
            half = xl if own else 1 - xl
            total = part[rows_of(first + (y * 2 + half) * w, w, w), PB].astype(F32)
            for d in range(3):
                total = total + ybin[i, rows_of(6 * OWN[c] + (2 * d + half) * w, w, w)].astype(F32)
            if own:
                ownb[i, pl.ds(OWN[c], w)] = total
            else:
                xb[i, pl.ds(OWN[c], w)] = total.astype(BF16)
                send(
                    xb.at[i, pl.ds(OWN[c], w)], xbin.at[i, pl.ds(OWN[c], w)],
                    rs_s.at[i, c], rs_r.at[i, c, 3], ldev,
                )

    def rs_final(c):
        first, w = CHUNKS[c][0], CHUNKS[c][1] // NT
        mine = pl.ds(OWN[c], w)
        for i in range(2):
            await_bytes(yain.at[i, pl.ds(3 * OWN[c], 3 * w)], rs_r.at[i, c, 2])
            await_bytes(xbin.at[i, mine], rs_r.at[i, c, 3])

        def store(sums, rows, columns):
            act, slope = gelu_pair(sums[1])
            hv[rows, columns] = (sums[0] * slope).astype(BF16)
            av[rows, columns] = act.astype(BF16)

        sums = []
        for i in range(2):
            total = ya[i, rows_of(4 * OWN[c] + y * w, w, w)].astype(F32)
            for d in range(3):
                total = total + yain[i, pl.ds(3 * OWN[c] + d * w, w)].astype(F32)
            sums.append(total)
        store(sums, rows_of(first + (xl * 4 + y) * w, w, w), PA)
        sums = [ownb[i, mine] + xbin[i, mine].astype(F32) for i in range(2)]
        store(sums, rows_of(first + (y * 2 + xl) * w, w, w), PB)

    def at_first(buf, i, c):
        first, w = CHUNKS[c][0], CHUNKS[c][1] // NT
        piece = buf.at[rows_of(first + (xl * 4 + y) * w, w, w), PA]
        for d in range(1, NY):
            send(piece, piece, at_s.at[i, c], at_r.at[i, c, 0], ydev(d))
        piece = buf.at[rows_of(first + (y * 2 + xl) * w, w, w), PB]
        send(piece, piece, at_s.at[i, c], at_r.at[i, c, 1], ldev)

    def at_second(buf, i, c):
        first, w = CHUNKS[c][0], CHUNKS[c][1] // NT
        await_bytes(buf.at[pl.ds(first, w), PB], at_r.at[i, c, 1])
        piece = buf.at[rows_of(first + y * 2 * w, 2 * w, w), PB]
        for d in range(1, NY):
            send(piece, piece, at_s.at[i, c], at_r.at[i, c, 3], ydev(d))
        await_bytes(buf.at[pl.ds(first, 3 * w), PA], at_r.at[i, c, 0])
        piece = buf.at[rows_of(first + xl * 4 * w, 4 * w, w), PA]
        send(piece, piece, at_s.at[i, c], at_r.at[i, c, 2], ldev)

    def at_wait(buf, i, c):
        first, w = CHUNKS[c][0], CHUNKS[c][1] // NT
        await_bytes(buf.at[pl.ds(first, 4 * w), PA], at_r.at[i, c, 2])
        await_bytes(buf.at[pl.ds(first, 6 * w), PB], at_r.at[i, c, 3])

    def grad_tile(left, right, out, n):
        block = lax.dot_general(
            left[:, 128 * n : 128 * (n + 1)], right[...], (((0,), (0,)), ((), ())), preferred_element_type=F32
        )
        out[pl.ds(128 * n, 128)] = block * FACTOR

    def grad_in(lo, hi):
        for n in range(lo, hi):
            grad_tile(mx, hv, gin, n)

    def grad_out(lo, hi):
        for n in range(lo, hi):
            grad_tile(av, ct, gout, n)

    def sc_sibling(part, sb, i, chunk):
        for dz in CHUNK_DZ[chunk]:
            send(part.at[pl.ds(POS[dz] + 64, 64)], sb.at[pl.ds(64 * dz, 64)], sc_s.at[i], sc_sib.at[i, dz], sib)

    def sc_piece(part, sb, q, rr, fin, i, dz, xr):
        rows = pl.ds(64 * dz + 32 * xr, 32)
        total = part[pl.ds(POS[dz] + 32 * xr, 32)].astype(F32) + sb[rows].astype(F32)
        if dz in (1, 2, 6, 7) or (dz, xr) in ((3, 0), (5, 1)):
            await_bytes(rr.at[rows], sc_ring.at[i, 2 * dz + xr])
            total = total + rr[rows].astype(F32)
        q[rows] = total.astype(BF16)
        way = 1 if dz < 4 or (dz == 4 and xr == 0) else -1
        if dz in (1, 7):
            slot = (0 if dz == 1 else 2) + xr
            dev = zxdev(way) if xr else zdev(way)
            send(q.at[rows], fin.at[slot], sc_s.at[i], sc_fin.at[i, slot], dev)
        else:
            to = 64 * (dz - way) + 32 * xr
            send(q.at[rows], rr.at[pl.ds(to, 32)], sc_s.at[i], sc_ring.at[i, 2 * (dz - way) + xr], zdev(way))

    def sc_chunk(part, sb, q, rr, fin, i, chunk):
        for dz in CHUNK_DZ[chunk]:
            await_bytes(sb.at[pl.ds(64 * dz, 64)], sc_sib.at[i, dz])
        if chunk == 4:
            order = [(4, 0), (4, 1)]
        else:
            order = [(chunk, 1), (NZ - chunk, 0), (chunk, 0), (NZ - chunk, 1)]
        for dz, xr in order:
            sc_piece(part, sb, q, rr, fin, i, dz, xr)

    def sc_own(part, sb, q, fin, i):
        await_bytes(sb.at[pl.ds(0, 64)], sc_sib.at[i, 0])
        q[pl.ds(32, 32)] = (part[pl.ds(32, 32)].astype(F32) + sb[pl.ds(32, 32)].astype(F32)).astype(BF16)
        send(q.at[pl.ds(32, 32)], fin.at[4], sc_s.at[i], sc_fin.at[i, 4], xdev)

    def sc_total(part, sb, fin, i):
        total = part[pl.ds(0, 32)].astype(F32) + sb[pl.ds(0, 32)].astype(F32)
        for slot in (4, 1, 3, 0, 2):
            await_bytes(fin.at[slot], sc_fin.at[i, slot])
            total = total + fin[slot].astype(F32)
        return total

    send(field_ref, halo.at[0], halo_s.at[0], halo_r.at[0], nxt)
    send(field_ref, halo.at[2], halo_s.at[1], halo_r.at[1], prv)
    ag_begin(ct, 0)
    await_bytes(halo.at[0], halo_r.at[0])
    await_bytes(halo.at[2], halo_r.at[1])

    def conv_tile(i, carry):
        lanes = pl.ds(pl.multiple_of(i * 128, 128), 128)
        rows = [halo[r, :, lanes].astype(F32) for r in range(3)]
        total = jnp.zeros((COLS, 128), F32)
        for k, (dr, dc) in enumerate(OFFSETS):
            moved = rows[1 + dr] if dc == 0 else pltpu.roll(rows[1 + dr], (-dc) % COLS, 0)
            total = total + taps_ref[k : k + 1, lanes] * moved
        mx[pl.ds(0, 32), lanes] = (rows[1] + total).astype(BF16)
        return carry

    lax.fori_loop(0, 8, conv_tile, 0)
    ag_cross(ct, 0)
    ag_begin(mx, 1)
    load_wo.wait()
    for c in range(5):
        if c > 0:
            ag_step(ct, 0, c)
        ag_ready(ct, 0, c)
        mm(ct, wo, gp, c, True)
        rs_first(gp, 0, c)
        if c > 0:
            ag_step(mx, 1, c)
        else:
            ag_cross(mx, 1)
            load_wi.wait()
        ag_ready(mx, 1, c)
        mm(mx, wi, hp, c, False)
        rs_first(hp, 1, c)
        if c > 0:
            rs_second(gp, 0, c - 1)
            rs_second(hp, 1, c - 1)
        if c > 1:
            rs_final(c - 2)
    rs_second(gp, 0, 4)
    rs_second(hp, 1, 4)

    def mgrad_part(c):
        at_wait(hv, 0, c)
        mm(hv, wi, pm, c, True)
        sc_sibling(pm, sbm, 0, c)

    def result_part(c):
        at_wait(av, 1, c)
        mm(av, wo, pr, c, False)
        sc_sibling(pr, sbr, 1, c)

    def mgrad_sum(c):
        sc_chunk(pm, sbm, qm, rrm, finm, 0, c)

    def result_sum(c):
        sc_chunk(pr, sbr, qr, rrr, finr, 1, c)

    def k_stage(i):
        if i == 0:
            send(mg, mhalo.at[0], mh_s.at[0], mh_r.at[0], nxt)
            send(mg, mhalo.at[1], mh_s.at[1], mh_r.at[1], prv)

            def kgrad_tile(n, carry):
                lanes = pl.ds(pl.multiple_of(n * 128, 128), 128)
                grad = mg[:, lanes]
                rows = [halo[r, :, lanes].astype(F32) for r in range(3)]
                sums = []
                for dr, dc in OFFSETS:
                    moved = rows[1 + dr] if dc == 0 else pltpu.roll(rows[1 + dr], (-dc) % COLS, 0)
                    sums.append(jnp.sum(grad * moved, axis=0, keepdims=True))
                kp[n] = jnp.concatenate(sums + [jnp.zeros((7, 128), F32)], axis=0)
                return carry

            lax.fori_loop(0, 8, kgrad_tile, 0)
            send(kp, kr, k_s.at[0], k_r.at[0], sib)
        if i == 1:
            await_bytes(kr, k_r.at[0])
            await_bytes(kp, k_s.at[0])
            kp[...] = kp[...] + kr[...]
            for n, d in enumerate(list(range(1, NZ)) + list(range(NZ))):
                dev = zdev(d) if n < 7 else zxdev(d)
                send(kp.at[(z + d) % NZ], kz.at[n], k_s.at[1], k_r.at[1], dev)
            await_bytes(mhalo.at[0], mh_r.at[0])
            await_bytes(mhalo.at[1], mh_r.at[1])

            def fgrad_tile(n, carry):
                lanes = pl.ds(pl.multiple_of(n * 128, 128), 128)
                rows = [mhalo[0, :, lanes], mg[:, lanes], mhalo[1, :, lanes]]
                total = rows[1]
                for k, (dr, dc) in enumerate(OFFSETS):
                    moved = rows[1 - dr] if dc == 0 else pltpu.roll(rows[1 - dr], dc % COLS, 0)
                    total = total + taps_ref[k : k + 1, lanes] * moved
                fgrad_ref[:, lanes] = total
                return carry

            lax.fori_loop(0, 8, fgrad_tile, 0)
        if i == 2:
            await_bytes(kz, k_r.at[1])
            total = kp[z]
            for n in range(15):
                total = total + kz[n]
            kf[...] = total
            kg[z] = total
            for d in range(1, NZ):
                send(kf, kg.at[z], k_s.at[2], k_r.at[2], zdev(d))
        if i == 3:
            await_bytes(kg.at[pl.ds(0, 7)], k_r.at[2])
            for n in range(8):
                kgrad_ref[:, 128 * n : 128 * (n + 1)] = kg[n, 0:9] * FACTOR

    at_first(hv, 0, 0)
    at_first(hv, 0, 1)
    at_first(hv, 0, 2)
    rs_final(3)
    rs_final(4)
    at_first(hv, 0, 4)
    at_first(hv, 0, 3)
    at_second(hv, 0, 0)
    at_second(hv, 0, 4)
    at_second(hv, 0, 3)
    at_first(av, 1, 4)
    at_second(hv, 0, 1)
    at_second(hv, 0, 2)
    at_first(av, 1, 3)
    mgrad_part(0)
    mgrad_part(4)
    sc_own(pm, sbm, qm, finm, 0)
    mgrad_sum(4)
    mgrad_part(1)
    mgrad_part(3)
    at_second(av, 1, 4)
    at_first(av, 1, 2)
    mgrad_sum(3)
    mgrad_part(2)
    at_second(av, 1, 3)
    at_first(av, 1, 1)
    result_part(4)
    mgrad_sum(2)
    result_sum(4)
    result_part(3)
    at_second(av, 1, 2)
    at_first(av, 1, 0)
    grad_in(0, 2)
    mgrad_sum(1)
    result_sum(3)
    result_part(2)
    at_second(av, 1, 1)
    mg[...] = sc_total(pm, sbm, finm, 0)
    k_stage(0)
    result_sum(2)
    result_part(1)
    k_stage(1)
    at_second(av, 1, 0)
    grad_in(2, 8)
    result_sum(1)
    k_stage(2)
    result_part(0)
    sc_own(pr, sbr, qr, finr, 1)
    grad_out(0, 7)
    result_ref[...] = sc_total(pr, sbr, finr, 1)
    k_stage(3)

    for i in range(2):
        await_bytes(halo.at[0], halo_s.at[i])
        await_bytes(mhalo.at[0], mh_s.at[i])
        await_bytes(ct.at[pl.ds(0, 992)], ag_s.at[i])
        for c in range(5):
            n = 7 * CHUNKS[c][1] // NT
            await_bytes(gp.at[pl.ds(0, n)], rs_s.at[i, c])
            await_bytes(hv.at[pl.ds(0, n)], at_s.at[i, c])
        await_bytes(pm.at[pl.ds(0, 992)], sc_s.at[i])
    await_bytes(kz, k_s.at[1])
    await_bytes(kg.at[pl.ds(0, 7)], k_s.at[2])


def write_out(*refs):
    copies = [pltpu.make_async_copy(refs[i], refs[5 + i], refs[10].at[i]) for i in range(5)]
    for cp in copies:
        cp.start()
    for cp in copies:
        cp.wait()


def on_device(field, w_in, w_out, taps, cotangent):
    vm, hbm = pl.BlockSpec(memory_space=pltpu.VMEM), pl.BlockSpec(memory_space=pl.ANY)
    dma = pltpu.SemaphoreType.DMA
    shapes = [
        ((COLS, DB), F32), ((COLS, DB), F32), ((9, DB), F32),
        ((DB, FB), F32), ((FB, DB), F32),
    ]
    scratch = [
        pltpu.VMEM((DB, FB), BF16), pltpu.VMEM((FB, DB), BF16),
        pltpu.VMEM((TOKENS, DB), BF16), pltpu.VMEM((TOKENS, DB), BF16),
        pltpu.VMEM((TOKENS, FB), BF16), pltpu.VMEM((TOKENS, FB), BF16),
        pltpu.VMEM((2, 512, CA), BF16), pltpu.VMEM((2, 512, CA), BF16), pltpu.VMEM((2, 384, CA), BF16),
        pltpu.VMEM((2, 768, CB), BF16), pltpu.VMEM((2, 128, CB), BF16), pltpu.VMEM((2, 128, CB), BF16),
        pltpu.VMEM((2, 128, CB), F32),
        pltpu.VMEM((TOKENS, FB), BF16), pltpu.VMEM((TOKENS, FB), BF16),
        pltpu.VMEM((TOKENS, DB), BF16), pltpu.VMEM((TOKENS, DB), BF16),
        pltpu.VMEM((512, DB), BF16), pltpu.VMEM((512, DB), BF16),
        pltpu.VMEM((512, DB), BF16), pltpu.VMEM((512, DB), BF16),
        pltpu.VMEM((512, DB), BF16), pltpu.VMEM((512, DB), BF16),
        pltpu.VMEM((5, 32, DB), BF16), pltpu.VMEM((5, 32, DB), BF16),
        pltpu.VMEM((3, COLS, DB), BF16), pltpu.VMEM((COLS, DB), F32), pltpu.VMEM((2, COLS, DB), F32),
        pltpu.VMEM((8, 16, 128), F32), pltpu.VMEM((8, 16, 128), F32), pltpu.VMEM((15, 16, 128), F32),
        pltpu.VMEM((16, 128), F32), pltpu.VMEM((8, 16, 128), F32),
        dma((2,)), dma((2,)), dma((2,)), dma((2,)), dma((2, 17)), dma((2, 8)),
        dma((2, 5)), dma((2, 5, 4)), dma((2, 5)), dma((2, 5, 4)),
        dma((2,)), dma((2, 8)), dma((2, 16)), dma((2, 5)), dma((2,)), dma((2,)), dma((3,)), dma((3,)),
    ]
    held = pl.pallas_call(
        kernel,
        out_shape=[pltpu.VMEM(*x) for x in shapes],
        in_specs=[vm, vm, vm, hbm, hbm],
        out_specs=[vm] * 5,
        scratch_shapes=scratch,
        compiler_params=pltpu.CompilerParams(
            collective_id=0, has_side_effects=True, vmem_limit_bytes=48 * 2**20
        ),
        cost_estimate=pl.CostEstimate(flops=6 * 2 * 1024 * 1024 * 896, bytes_accessed=12 * 2**20, transcendentals=0),
        name="block",
    )(field.reshape(COLS, DB), cotangent.reshape(COLS, DB), taps, w_in, w_out)
    result, fgrad, kgrad, grad_in, grad_out = pl.pallas_call(
        write_out,
        out_shape=[jax.ShapeDtypeStruct(*x) for x in shapes],
        in_specs=[hbm] * 5,
        out_specs=[pl.BlockSpec(memory_space=pltpu.HBM)] * 5,
        scratch_shapes=[dma((5,))],
        compiler_params=pltpu.CompilerParams(vmem_limit_bytes=2**20),
        name="write_out",
    )(*held)
    return (result.reshape(1, COLS, DB), fgrad.reshape(1, COLS, DB), grad_in, grad_out, kgrad)


def solution(mesh):
    space = P("space", None, "tensor")
    return jax.shard_map(
        on_device,
        mesh=mesh,
        in_specs=(space, P("tensor", "space"), P("space", "tensor"), P(None, "tensor"), space),
        out_specs=(space, space, P("tensor", "space"), P("space", "tensor"), P(None, "tensor")),
        check_vma=False,
    )
```

time: 140 us -> 110 us (0.79)
  Pallas kernels: 126 us -> 109 us
  matrix products: 10.5 us -> 0 us
  local copies, waits for them, and re-layouts: 1.96 us -> 0 us
    pallas_call x1 -> x2, Pallas kernels: 126 us -> 109 us  [the longest x1 106 us: on_device(): pl.pallas_call(kernel, out_shape=[pltpu.VMEM(*x) for x in shapes], in_spe...]
    dot_general x2 -> x0, matrix products: 10.5 us -> none  [the longest x1 6.5 us: on_device(): jnp.einsum('td,tf->df', mixed, hgrads, preferred_element_type=F32) * FACTOR]
    unnamed x13 -> x0, local copies, waits for them, and re-layouts: 1.96 us -> none
where the time goes in v2:
time: 110 us
  Pallas kernels  109 us (99%)
    pallas_call x1, Pallas kernels, on_device(): pl.pallas_call(kernel, out_shape=[pltpu.VMEM(*x) for x in shapes], in_spe...  106 us
    pallas_call x1, Pallas kernels, on_device(): pl.pallas_call(write_out, out_shape=[jax.ShapeDtypeStruct(*x) for x in sh...  3.2 us

profile of v2, /device:TPU:1, one launch (start us, length us, event | category | flops | bytes accessed | tf_op | source)
XLA Modules:
  0.0 110.0 jit_solution(3475843320063617990)
XLA Ops:
  0.6 106.0 %block.1 = (f32[32,1024]{1,0:T(8,128)S(1)}, f32[32,1024]{1,0:T(8,128)S(1)}, f32[9,1024]{1,0:T(8,128)S(1)}, f32[1024,896]{1,0:T(8,128)S(1)}, f32[896,1024]{1,0:T(8,128)S(1)}) custom-call(bf16[32,1024]{1,0:T(8,128)(2,1)} %bitcast.6, bf16[32,1024]{1,0:T(8,128)(2,1)} %bitcast.7, f32[9,1024]{1,0:T(8,128)} %taps_ref.1, bf16[1024,896]{1,0:T(8,128)(2,1)} %wi_hbm.1, ...), custom_call_target="tpu_custom_call" | custom-call | flops 11274289152 | bytes 12582912 | tf_op jit(solution)/shard_map/block/pallas_call | solution.py:486
  106.7 3.2 %write_out.1 = (f32[32,1024]{1,0:T(8,128)}, f32[32,1024]{1,0:T(8,128)}, f32[9,1024]{1,0:T(8,128)}, f32[1024,896]{1,0:T(8,128)}, f32[896,1024]{1,0:T(8,128)}) custom-call(f32[32,1024]{1,0:T(8,128)S(1)} %get-tuple-element.15.refs_0_, f32[32,1024]{1,0:T(8,128)S(1)} %get-tuple-element.16.refs_1_, f32[9,1024]{1,0:T(8,128)S(1)} %get-tuple-element.17.refs_2_, ...), custom_call_target="tpu_custom_call" | custom-call | tf_op jit(solution)/shard_map/write_out/pallas_call | solution.py:498

commit v3 on v2

--- a/solution.py
+++ b/solution.py
@@ -21,6 +21,7 @@
 CHUNKS = [(0, 128), (128, 256), (384, 256), (640, 256), (896, 128)]
 CHUNK_DZ = [[0], [1, 7], [2, 6], [3, 5], [4]]
 OWN = [0, 16, 48, 80, 112]
+RING = [(3, 0), (5, 1)] + [(dz, xr) for dz in (1, 2, 6, 7) for xr in range(2)]
 CA = 512
 CB = FB - CA
 PA, PB = pl.ds(0, CA), pl.ds(CA, CB)
@@ -36,9 +37,9 @@
 
 
 def kernel(
-    field_ref, cot_ref, taps_ref, wi_hbm, wo_hbm,
+    field_hbm, cot_hbm, taps_hbm, wi_hbm, wo_hbm,
     result_ref, fgrad_ref, kgrad_ref, gin, gout,
-    wi, wo, ct, mx, gp, hp, xa, ya, yain, ybin, xb, xbin, ownb, av, hv,
+    taps_ref, wi, wo, ct, mx, gp, hp, xa, ya, yain, ybin, xb, xbin, ownb, av, hv,
     pm, pr, sbm, sbr, qm, qr, rrm, rrr, finm, finr, halo, mg, mhalo,
     kp, kr, kz, kf, kg,
     lsem, halo_s, halo_r, ag_s, ag_r, sib_r, rs_s, rs_r, at_s, at_r,
@@ -72,6 +73,13 @@
 
     load_wi = pltpu.make_async_copy(wi_hbm, wi, lsem.at[0])
     load_wo = pltpu.make_async_copy(wo_hbm, wo, lsem.at[1])
+    loads = [
+        pltpu.make_async_copy(cot_hbm, ct.at[pl.ds(0, 32)], lsem.at[2]),
+        pltpu.make_async_copy(field_hbm, halo.at[1], lsem.at[3]),
+        pltpu.make_async_copy(taps_hbm, taps_ref, lsem.at[4]),
+    ]
+    for cp in loads:
+        cp.start()
     load_wo.start()
     load_wi.start()
 
@@ -80,8 +88,8 @@
     barrier = pltpu.get_barrier_semaphore()
     for dev in partners:
         pl.semaphore_signal(barrier, inc=1, device_id=dev, device_id_type=MESH)
-    ct[pl.ds(0, 32)] = cot_ref[...]
-    halo[1] = field_ref[...]
+    for cp in loads:
+        cp.wait()
     pl.semaphore_wait(barrier, len(partners))
 
     def ag_begin(buf, i):
@@ -111,11 +119,10 @@
                         ag_r.at[i, 4 * j + 1 + 2 * xr + way], zdev(ahead),
                     )
         for dz in CHUNK_DZ[j]:
-            send(buf.at[pl.ds(POS[dz], 64)], buf.at[pl.ds(POS[dz] + 64, 64)], ag_s.at[i], sib_r.at[i, dz], sib)
+            send(buf.at[pl.ds(POS[dz], 64)], buf.at[pl.ds(POS[dz] + 64, 64)], ag_s.at[i], sib_r.at[i, j], sib)
 
     def ag_ready(buf, i, j):
-        for dz in CHUNK_DZ[j]:
-            await_bytes(buf.at[pl.ds(POS[dz] + 64, 64)], sib_r.at[i, dz])
+        await_bytes(buf.at[pl.ds(0, CHUNKS[j][1] // 2)], sib_r.at[i, j])
 
     def mm(src, w, out, chunk, transposed):
         first, length = CHUNKS[chunk]
@@ -134,29 +141,28 @@
         first, w = CHUNKS[c][0], CHUNKS[c][1] // NT
         send(
             part.at[rows_of(first + (1 - xl) * 4 * w, 4 * w, w), PA], xa.at[i, pl.ds(4 * OWN[c], 4 * w)],
-            rs_s.at[i, c], rs_r.at[i, c, 0], ldev,
+            rs_s.at[i], rs_r.at[i, c], ldev,
         )
         for d in range(1, NY):
             to = (y + d) % NY
             send(
                 part.at[rows_of(first + to * 2 * w, 2 * w, w), PB],
                 ybin.at[i, pl.ds(6 * OWN[c] + (d - 1) * 2 * w, 2 * w)],
-                rs_s.at[i, c], rs_r.at[i, c, 1], ydev(d),
+                rs_s.at[i], rs_r.at[i, c], ydev(d),
             )
 
     def rs_second(part, i, c):
         first, w = CHUNKS[c][0], CHUNKS[c][1] // NT
         got = xa.at[i, pl.ds(4 * OWN[c], 4 * w)]
-        await_bytes(got, rs_r.at[i, c, 0])
+        await_bytes(gp.at[pl.ds(0, 17 * w), pl.ds(0, 256)], rs_r.at[i, c])
         mine = part[rows_of(first + xl * 4 * w, 4 * w, w), PA].astype(F32)
         ya[i, pl.ds(4 * OWN[c], 4 * w)] = (mine + got[...].astype(F32)).astype(BF16)
         for d in range(1, NY):
             to = (y + d) % NY
             send(
                 ya.at[i, rows_of(4 * OWN[c] + to * w, w, w)], yain.at[i, pl.ds(3 * OWN[c] + (d - 1) * w, w)],
-                rs_s.at[i, c], rs_r.at[i, c, 2], ydev(d),
+                rs_s.at[i], rs_r.at[2, c], ydev(d),
             )
-        await_bytes(ybin.at[i, pl.ds(6 * OWN[c], 6 * w)], rs_r.at[i, c, 1])
         for own in range(2):
             half = xl if own else 1 - xl
             total = part[rows_of(first + (y * 2 + half) * w, w, w), PB].astype(F32)
@@ -168,15 +174,13 @@
                 xb[i, pl.ds(OWN[c], w)] = total.astype(BF16)
                 send(
                     xb.at[i, pl.ds(OWN[c], w)], xbin.at[i, pl.ds(OWN[c], w)],
-                    rs_s.at[i, c], rs_r.at[i, c, 3], ldev,
+                    rs_s.at[i], rs_r.at[2, c], ldev,
                 )
 
     def rs_final(c):
         first, w = CHUNKS[c][0], CHUNKS[c][1] // NT
         mine = pl.ds(OWN[c], w)
-        for i in range(2):
-            await_bytes(yain.at[i, pl.ds(3 * OWN[c], 3 * w)], rs_r.at[i, c, 2])
-            await_bytes(xbin.at[i, mine], rs_r.at[i, c, 3])
+        await_bytes(gp.at[pl.ds(0, 15 * w), pl.ds(0, 256)], rs_r.at[2, c])
 
         def store(sums, rows, columns):
             act, slope = gelu_pair(sums[1])
@@ -197,24 +201,22 @@
         first, w = CHUNKS[c][0], CHUNKS[c][1] // NT
         piece = buf.at[rows_of(first + (xl * 4 + y) * w, w, w), PA]
         for d in range(1, NY):
-            send(piece, piece, at_s.at[i, c], at_r.at[i, c, 0], ydev(d))
+            send(piece, piece, at_s.at[i], at_r.at[i, c, 0], ydev(d))
         piece = buf.at[rows_of(first + (y * 2 + xl) * w, w, w), PB]
-        send(piece, piece, at_s.at[i, c], at_r.at[i, c, 1], ldev)
+        send(piece, piece, at_s.at[i], at_r.at[i, c, 0], ldev)
 
     def at_second(buf, i, c):
         first, w = CHUNKS[c][0], CHUNKS[c][1] // NT
-        await_bytes(buf.at[pl.ds(first, w), PB], at_r.at[i, c, 1])
+        await_bytes(gp.at[pl.ds(0, 5 * w), PB], at_r.at[i, c, 0])
         piece = buf.at[rows_of(first + y * 2 * w, 2 * w, w), PB]
         for d in range(1, NY):
-            send(piece, piece, at_s.at[i, c], at_r.at[i, c, 3], ydev(d))
-        await_bytes(buf.at[pl.ds(first, 3 * w), PA], at_r.at[i, c, 0])
+            send(piece, piece, at_s.at[i], at_r.at[i, c, 1], ydev(d))
         piece = buf.at[rows_of(first + xl * 4 * w, 4 * w, w), PA]
-        send(piece, piece, at_s.at[i, c], at_r.at[i, c, 2], ldev)
+        send(piece, piece, at_s.at[i], at_r.at[i, c, 1], ldev)
 
     def at_wait(buf, i, c):
         first, w = CHUNKS[c][0], CHUNKS[c][1] // NT
-        await_bytes(buf.at[pl.ds(first, 4 * w), PA], at_r.at[i, c, 2])
-        await_bytes(buf.at[pl.ds(first, 6 * w), PB], at_r.at[i, c, 3])
+        await_bytes(gp.at[pl.ds(0, 17 * w), pl.ds(0, 256)], at_r.at[i, c, 1])
 
     def grad_tile(left, right, out, n):
         block = lax.dot_general(
@@ -232,51 +234,46 @@
 
     def sc_sibling(part, sb, i, chunk):
         for dz in CHUNK_DZ[chunk]:
-            send(part.at[pl.ds(POS[dz] + 64, 64)], sb.at[pl.ds(64 * dz, 64)], sc_s.at[i], sc_sib.at[i, dz], sib)
+            send(part.at[pl.ds(POS[dz] + 64, 64)], sb.at[pl.ds(64 * dz, 64)], sc_s.at[i], sc_sib.at[i, chunk], sib)
 
     def sc_piece(part, sb, q, rr, fin, i, dz, xr):
         rows = pl.ds(64 * dz + 32 * xr, 32)
         total = part[pl.ds(POS[dz] + 32 * xr, 32)].astype(F32) + sb[rows].astype(F32)
-        if dz in (1, 2, 6, 7) or (dz, xr) in ((3, 0), (5, 1)):
-            await_bytes(rr.at[rows], sc_ring.at[i, 2 * dz + xr])
+        if (dz, xr) in RING:
+            await_bytes(rr.at[rows], sc_ring.at[i, RING.index((dz, xr))])
             total = total + rr[rows].astype(F32)
         q[rows] = total.astype(BF16)
         way = 1 if dz < 4 or (dz == 4 and xr == 0) else -1
         if dz in (1, 7):
             slot = (0 if dz == 1 else 2) + xr
             dev = zxdev(way) if xr else zdev(way)
-            send(q.at[rows], fin.at[slot], sc_s.at[i], sc_fin.at[i, slot], dev)
+            send(q.at[rows], fin.at[slot], sc_s.at[i], sc_fin.at[i], dev)
         else:
             to = 64 * (dz - way) + 32 * xr
-            send(q.at[rows], rr.at[pl.ds(to, 32)], sc_s.at[i], sc_ring.at[i, 2 * (dz - way) + xr], zdev(way))
-
-    def sc_chunk(part, sb, q, rr, fin, i, chunk):
-        for dz in CHUNK_DZ[chunk]:
-            await_bytes(sb.at[pl.ds(64 * dz, 64)], sc_sib.at[i, dz])
-        if chunk == 4:
-            order = [(4, 0), (4, 1)]
-        else:
-            order = [(chunk, 1), (NZ - chunk, 0), (chunk, 0), (NZ - chunk, 1)]
-        for dz, xr in order:
+            send(q.at[rows], rr.at[pl.ds(to, 32)], sc_s.at[i], sc_ring.at[i, RING.index((dz - way, xr))], zdev(way))
+
+    def sc_chunk(part, sb, q, rr, fin, i, chunk, late):
+        if not late:
+            await_bytes(sb.at[pl.ds(0, CHUNKS[chunk][1] // 2)], sc_sib.at[i, chunk])
+        for dz, xr in ((chunk, 1 - late), (NZ - chunk, late)):
             sc_piece(part, sb, q, rr, fin, i, dz, xr)
 
     def sc_own(part, sb, q, fin, i):
         await_bytes(sb.at[pl.ds(0, 64)], sc_sib.at[i, 0])
         q[pl.ds(32, 32)] = (part[pl.ds(32, 32)].astype(F32) + sb[pl.ds(32, 32)].astype(F32)).astype(BF16)
-        send(q.at[pl.ds(32, 32)], fin.at[4], sc_s.at[i], sc_fin.at[i, 4], xdev)
+        send(q.at[pl.ds(32, 32)], fin.at[4], sc_s.at[i], sc_fin.at[i], xdev)
 
     def sc_total(part, sb, fin, i):
         total = part[pl.ds(0, 32)].astype(F32) + sb[pl.ds(0, 32)].astype(F32)
-        for slot in (4, 1, 3, 0, 2):
-            await_bytes(fin.at[slot], sc_fin.at[i, slot])
+        await_bytes(fin, sc_fin.at[i])
+        for slot in range(5):
             total = total + fin[slot].astype(F32)
         return total
 
-    send(field_ref, halo.at[0], halo_s.at[0], halo_r.at[0], nxt)
-    send(field_ref, halo.at[2], halo_s.at[1], halo_r.at[1], prv)
+    send(halo.at[1], halo.at[0], halo_s, halo_r, nxt)
+    send(halo.at[1], halo.at[2], halo_s, halo_r, prv)
     ag_begin(ct, 0)
-    await_bytes(halo.at[0], halo_r.at[0])
-    await_bytes(halo.at[2], halo_r.at[1])
+    await_bytes(halo.at[pl.ds(0, 2)], halo_r)
 
     def conv_tile(i, carry):
         lanes = pl.ds(pl.multiple_of(i * 128, 128), 128)
@@ -292,12 +289,14 @@
     ag_cross(ct, 0)
     ag_begin(mx, 1)
     load_wo.wait()
-    for c in range(5):
+    def cot_chunk(c):
         if c > 0:
             ag_step(ct, 0, c)
         ag_ready(ct, 0, c)
         mm(ct, wo, gp, c, True)
         rs_first(gp, 0, c)
+
+    def mixed_chunk(c):
         if c > 0:
             ag_step(mx, 1, c)
         else:
@@ -306,6 +305,12 @@
         ag_ready(mx, 1, c)
         mm(mx, wi, hp, c, False)
         rs_first(hp, 1, c)
+
+    cot_chunk(0)
+    for c in range(5):
+        if c < 4:
+            cot_chunk(c + 1)
+        mixed_chunk(c)
         if c > 0:
             rs_second(gp, 0, c - 1)
             rs_second(hp, 1, c - 1)
@@ -324,16 +329,16 @@
         mm(av, wo, pr, c, False)
         sc_sibling(pr, sbr, 1, c)
 
-    def mgrad_sum(c):
-        sc_chunk(pm, sbm, qm, rrm, finm, 0, c)
-
-    def result_sum(c):
-        sc_chunk(pr, sbr, qr, rrr, finr, 1, c)
+    def mgrad_sum(c, late):
+        sc_chunk(pm, sbm, qm, rrm, finm, 0, c, late)
+
+    def result_sum(c, late):
+        sc_chunk(pr, sbr, qr, rrr, finr, 1, c, late)
 
     def k_stage(i):
         if i == 0:
-            send(mg, mhalo.at[0], mh_s.at[0], mh_r.at[0], nxt)
-            send(mg, mhalo.at[1], mh_s.at[1], mh_r.at[1], prv)
+            send(mg, mhalo.at[0], mh_s, mh_r, nxt)
+            send(mg, mhalo.at[1], mh_s, mh_r, prv)
 
             def kgrad_tile(n, carry):
                 lanes = pl.ds(pl.multiple_of(n * 128, 128), 128)
@@ -352,11 +357,10 @@
             await_bytes(kr, k_r.at[0])
             await_bytes(kp, k_s.at[0])
             kp[...] = kp[...] + kr[...]
-            for n, d in enumerate(list(range(1, NZ)) + list(range(NZ))):
-                dev = zdev(d) if n < 7 else zxdev(d)
-                send(kp.at[(z + d) % NZ], kz.at[n], k_s.at[1], k_r.at[1], dev)
-            await_bytes(mhalo.at[0], mh_r.at[0])
-            await_bytes(mhalo.at[1], mh_r.at[1])
+            for d in range(1, NZ):
+                send(kp.at[(z + d) % NZ], kz.at[d - 1], k_s.at[1], k_r.at[1], zdev(d))
+        if i == 4:
+            await_bytes(mhalo, mh_r)
 
             def fgrad_tile(n, carry):
                 lanes = pl.ds(pl.multiple_of(n * 128, 128), 128)
@@ -372,16 +376,18 @@
         if i == 2:
             await_bytes(kz, k_r.at[1])
             total = kp[z]
-            for n in range(15):
+            for n in range(7):
                 total = total + kz[n]
             kf[...] = total
             kg[z] = total
-            for d in range(1, NZ):
-                send(kf, kg.at[z], k_s.at[2], k_r.at[2], zdev(d))
+            for d in range(NZ):
+                if d > 0:
+                    send(kf, kg.at[z], k_s.at[2], k_r.at[2], zdev(d))
+                send(kf, kg.at[NZ + z], k_s.at[2], k_r.at[2], zxdev(d))
         if i == 3:
-            await_bytes(kg.at[pl.ds(0, 7)], k_r.at[2])
+            await_bytes(kg.at[pl.ds(0, 15)], k_r.at[2])
             for n in range(8):
-                kgrad_ref[:, 128 * n : 128 * (n + 1)] = kg[n, 0:9] * FACTOR
+                kgrad_ref[:, 128 * n : 128 * (n + 1)] = (kg[n, 0:9] + kg[NZ + n, 0:9]) * FACTOR
 
     at_first(hv, 0, 0)
     at_first(hv, 0, 1)
@@ -391,61 +397,67 @@
     at_first(hv, 0, 4)
     at_first(hv, 0, 3)
     at_second(hv, 0, 0)
+    at_second(hv, 0, 1)
     at_second(hv, 0, 4)
     at_second(hv, 0, 3)
     at_first(av, 1, 4)
-    at_second(hv, 0, 1)
     at_second(hv, 0, 2)
     at_first(av, 1, 3)
+    at_first(av, 1, 2)
     mgrad_part(0)
     mgrad_part(4)
     sc_own(pm, sbm, qm, finm, 0)
-    mgrad_sum(4)
-    mgrad_part(1)
+    mgrad_sum(4, 0)
     mgrad_part(3)
     at_second(av, 1, 4)
-    at_first(av, 1, 2)
-    mgrad_sum(3)
+    mgrad_sum(3, 0)
+    at_first(av, 1, 1)
     mgrad_part(2)
+    mgrad_sum(3, 1)
     at_second(av, 1, 3)
-    at_first(av, 1, 1)
+    mgrad_sum(2, 0)
+    at_first(av, 1, 0)
+    mgrad_part(1)
+    mgrad_sum(2, 1)
+    at_second(av, 1, 2)
     result_part(4)
-    mgrad_sum(2)
-    result_sum(4)
+    mgrad_sum(1, 0)
+    result_sum(4, 0)
+    at_second(av, 1, 1)
+    mgrad_sum(1, 1)
     result_part(3)
-    at_second(av, 1, 2)
-    at_first(av, 1, 0)
+    result_sum(3, 0)
+    at_second(av, 1, 0)
     grad_in(0, 2)
-    mgrad_sum(1)
-    result_sum(3)
-    result_part(2)
-    at_second(av, 1, 1)
+    result_sum(3, 1)
     mg[...] = sc_total(pm, sbm, finm, 0)
     k_stage(0)
-    result_sum(2)
+    result_part(2)
+    k_stage(1)
+    result_sum(2, 0)
     result_part(1)
-    k_stage(1)
-    at_second(av, 1, 0)
-    grad_in(2, 8)
-    result_sum(1)
+    result_sum(2, 1)
+    result_part(0)
     k_stage(2)
-    result_part(0)
     sc_own(pr, sbr, qr, finr, 1)
+    result_sum(1, 0)
+    k_stage(4)
+    grad_in(2, 4)
+    result_sum(1, 1)
+    grad_in(4, 8)
     grad_out(0, 7)
+    k_stage(3)
     result_ref[...] = sc_total(pr, sbr, finr, 1)
-    k_stage(3)
-
+
+    await_bytes(halo.at[pl.ds(0, 2)], halo_s)
+    await_bytes(mhalo, mh_s)
     for i in range(2):
-        await_bytes(halo.at[0], halo_s.at[i])
-        await_bytes(mhalo.at[0], mh_s.at[i])
         await_bytes(ct.at[pl.ds(0, 992)], ag_s.at[i])
-        for c in range(5):
-            n = 7 * CHUNKS[c][1] // NT
-            await_bytes(gp.at[pl.ds(0, n)], rs_s.at[i, c])
-            await_bytes(hv.at[pl.ds(0, n)], at_s.at[i, c])
+        await_bytes(gp.at[pl.ds(0, 896)], rs_s.at[i])
+        await_bytes(hv.at[pl.ds(0, 896)], at_s.at[i])
         await_bytes(pm.at[pl.ds(0, 992)], sc_s.at[i])
     await_bytes(kz, k_s.at[1])
-    await_bytes(kg.at[pl.ds(0, 7)], k_s.at[2])
+    await_bytes(kg.at[pl.ds(0, 15)], k_s.at[2])
 
 
 def write_out(*refs):
@@ -464,7 +476,7 @@
         ((DB, FB), F32), ((FB, DB), F32),
     ]
     scratch = [
-        pltpu.VMEM((DB, FB), BF16), pltpu.VMEM((FB, DB), BF16),
+        pltpu.VMEM((9, DB), F32), pltpu.VMEM((DB, FB), BF16), pltpu.VMEM((FB, DB), BF16),
         pltpu.VMEM((TOKENS, DB), BF16), pltpu.VMEM((TOKENS, DB), BF16),
         pltpu.VMEM((TOKENS, FB), BF16), pltpu.VMEM((TOKENS, FB), BF16),
         pltpu.VMEM((2, 512, CA), BF16), pltpu.VMEM((2, 512, CA), BF16), pltpu.VMEM((2, 384, CA), BF16),
@@ -477,16 +489,16 @@
         pltpu.VMEM((512, DB), BF16), pltpu.VMEM((512, DB), BF16),
         pltpu.VMEM((5, 32, DB), BF16), pltpu.VMEM((5, 32, DB), BF16),
         pltpu.VMEM((3, COLS, DB), BF16), pltpu.VMEM((COLS, DB), F32), pltpu.VMEM((2, COLS, DB), F32),
-        pltpu.VMEM((8, 16, 128), F32), pltpu.VMEM((8, 16, 128), F32), pltpu.VMEM((15, 16, 128), F32),
-        pltpu.VMEM((16, 128), F32), pltpu.VMEM((8, 16, 128), F32),
-        dma((2,)), dma((2,)), dma((2,)), dma((2,)), dma((2, 17)), dma((2, 8)),
-        dma((2, 5)), dma((2, 5, 4)), dma((2, 5)), dma((2, 5, 4)),
-        dma((2,)), dma((2, 8)), dma((2, 16)), dma((2, 5)), dma((2,)), dma((2,)), dma((3,)), dma((3,)),
+        pltpu.VMEM((8, 16, 128), F32), pltpu.VMEM((8, 16, 128), F32), pltpu.VMEM((7, 16, 128), F32),
+        pltpu.VMEM((16, 128), F32), pltpu.VMEM((16, 16, 128), F32),
+        dma((5,)), dma, dma, dma((2,)), dma((2, 17)), dma((2, 5)),
+        dma((2,)), dma((3, 5)), dma((2,)), dma((2, 5, 2)),
+        dma((2,)), dma((2, 5)), dma((2, len(RING))), dma((2,)), dma, dma, dma((3,)), dma((3,)),
     ]
     held = pl.pallas_call(
         kernel,
         out_shape=[pltpu.VMEM(*x) for x in shapes],
-        in_specs=[vm, vm, vm, hbm, hbm],
+        in_specs=[hbm] * 5,
         out_specs=[vm] * 5,
         scratch_shapes=scratch,
         compiler_params=pltpu.CompilerParams(

time: 110 us -> 101 us (0.918)
  Pallas kernels: 109 us -> 101 us
    pallas_call x1, Pallas kernels: 106 us -> 97.4 us  [on_device(): pl.pallas_call(kernel, out_shape=[pltpu.VMEM(*x) for x in shapes], in_spe...]
where the time goes in v3:
time: 101 us
  Pallas kernels  101 us (100%)
    pallas_call x1, Pallas kernels, on_device(): pl.pallas_call(kernel, out_shape=[pltpu.VMEM(*x) for x in shapes], in_spe...  97.4 us
    pallas_call x1, Pallas kernels, on_device(): pl.pallas_call(write_out, out_shape=[jax.ShapeDtypeStruct(*x) for x in sh...  3.2 us

profile of v3, /device:TPU:1, one launch (start us, length us, event | category | flops | bytes accessed | tf_op | source)
XLA Modules:
  0.0 101.4 jit_solution(5985498380414091333)
XLA Ops:
  0.6 97.4 %block.1 = (f32[32,1024]{1,0:T(8,128)S(1)}, f32[32,1024]{1,0:T(8,128)S(1)}, f32[9,1024]{1,0:T(8,128)S(1)}, f32[1024,896]{1,0:T(8,128)S(1)}, f32[896,1024]{1,0:T(8,128)S(1)}) custom-call(bf16[32,1024]{1,0:T(8,128)(2,1)} %bitcast.6, bf16[32,1024]{1,0:T(8,128)(2,1)} %bitcast.7, f32[9,1024]{1,0:T(8,128)} %taps_hbm.1, bf16[1024,896]{1,0:T(8,128)(2,1)} %wi_hbm.1, ...), custom_call_target="tpu_custom_call" | custom-call | flops 11274289152 | bytes 12582912 | tf_op jit(solution)/shard_map/block/pallas_call | solution.py:498
  98.1 3.2 %write_out.1 = (f32[32,1024]{1,0:T(8,128)}, f32[32,1024]{1,0:T(8,128)}, f32[9,1024]{1,0:T(8,128)}, f32[1024,896]{1,0:T(8,128)}, f32[896,1024]{1,0:T(8,128)}) custom-call(f32[32,1024]{1,0:T(8,128)S(1)} %get-tuple-element.15.refs_0_, f32[32,1024]{1,0:T(8,128)S(1)} %get-tuple-element.16.refs_1_, f32[9,1024]{1,0:T(8,128)S(1)} %get-tuple-element.17.refs_2_, ...), custom_call_target="tpu_custom_call" | custom-call | tf_op jit(solution)/shard_map/write_out/pallas_call | solution.py:510

commit v4 on v3

--- a/solution.py
+++ b/solution.py
@@ -83,8 +83,7 @@
     load_wo.start()
     load_wi.start()
 
-    partners = [ydev(d) for d in range(1, NY)] + [zdev(d) for d in range(1, NZ)]
-    partners += [zxdev(d) for d in range(NZ)] + [ldev, nxt, prv]
+    partners = [ydev(d) for d in range(1, NY)] + [zdev(1), zdev(-1), ldev, xdev, nxt, prv]
     barrier = pltpu.get_barrier_semaphore()
     for dev in partners:
         pl.semaphore_signal(barrier, inc=1, device_id=dev, device_id_type=MESH)
@@ -404,6 +403,8 @@
     at_second(hv, 0, 2)
     at_first(av, 1, 3)
     at_first(av, 1, 2)
+    at_first(av, 1, 1)
+    at_first(av, 1, 0)
     mgrad_part(0)
     mgrad_part(4)
     sc_own(pm, sbm, qm, finm, 0)
@@ -411,23 +412,21 @@
     mgrad_part(3)
     at_second(av, 1, 4)
     mgrad_sum(3, 0)
-    at_first(av, 1, 1)
     mgrad_part(2)
     mgrad_sum(3, 1)
     at_second(av, 1, 3)
     mgrad_sum(2, 0)
-    at_first(av, 1, 0)
+    at_second(av, 1, 2)
     mgrad_part(1)
     mgrad_sum(2, 1)
-    at_second(av, 1, 2)
     result_part(4)
+    at_second(av, 1, 1)
     mgrad_sum(1, 0)
     result_sum(4, 0)
-    at_second(av, 1, 1)
+    at_second(av, 1, 0)
     mgrad_sum(1, 1)
     result_part(3)
     result_sum(3, 0)
-    at_second(av, 1, 0)
     grad_in(0, 2)
     result_sum(3, 1)
     mg[...] = sc_total(pm, sbm, finm, 0)
@@ -438,13 +437,14 @@
     result_part(1)
     result_sum(2, 1)
     result_part(0)
+    grad_in(2, 4)
+    sc_own(pr, sbr, qr, finr, 1)
+    grad_in(4, 6)
     k_stage(2)
-    sc_own(pr, sbr, qr, finr, 1)
     result_sum(1, 0)
     k_stage(4)
-    grad_in(2, 4)
     result_sum(1, 1)
-    grad_in(4, 8)
+    grad_in(6, 8)
     grad_out(0, 7)
     k_stage(3)
     result_ref[...] = sc_total(pr, sbr, finr, 1)

time: 101 us -> 101 us (level)
  Pallas kernels: 101 us -> 99.9 us
where the time goes in v4:
time: 101 us
  Pallas kernels  99.9 us (99%)
    pallas_call x1, Pallas kernels, on_device(): pl.pallas_call(kernel, out_shape=[pltpu.VMEM(*x) for x in shapes], in_spe...  96.7 us
    pallas_call x1, Pallas kernels, on_device(): pl.pallas_call(write_out, out_shape=[jax.ShapeDtypeStruct(*x) for x in sh...  3.2 us

profile of v4, /device:TPU:1, one launch (start us, length us, event | category | flops | bytes accessed | tf_op | source)
XLA Modules:
  0.0 100.7 jit_solution(12222811704526452997)
XLA Ops:
  0.6 96.7 %block.1 = (f32[32,1024]{1,0:T(8,128)S(1)}, f32[32,1024]{1,0:T(8,128)S(1)}, f32[9,1024]{1,0:T(8,128)S(1)}, f32[1024,896]{1,0:T(8,128)S(1)}, f32[896,1024]{1,0:T(8,128)S(1)}) custom-call(bf16[32,1024]{1,0:T(8,128)(2,1)} %bitcast.6, bf16[32,1024]{1,0:T(8,128)(2,1)} %bitcast.7, f32[9,1024]{1,0:T(8,128)} %taps_hbm.1, bf16[1024,896]{1,0:T(8,128)(2,1)} %wi_hbm.1, ...), custom_call_target="tpu_custom_call" | custom-call | flops 11274289152 | bytes 12582912 | tf_op jit(solution)/shard_map/block/pallas_call | solution.py:498
  97.3 3.2 %write_out.1 = (f32[32,1024]{1,0:T(8,128)}, f32[32,1024]{1,0:T(8,128)}, f32[9,1024]{1,0:T(8,128)}, f32[1024,896]{1,0:T(8,128)}, f32[896,1024]{1,0:T(8,128)}) custom-call(f32[32,1024]{1,0:T(8,128)S(1)} %get-tuple-element.15.refs_0_, f32[32,1024]{1,0:T(8,128)S(1)} %get-tuple-element.16.refs_1_, f32[9,1024]{1,0:T(8,128)S(1)} %get-tuple-element.17.refs_2_, ...), custom_call_target="tpu_custom_call" | custom-call | tf_op jit(solution)/shard_map/write_out/pallas_call | solution.py:510

commit v5 on v4

--- a/solution.py
+++ b/solution.py
@@ -21,7 +21,7 @@
 CHUNKS = [(0, 128), (128, 256), (384, 256), (640, 256), (896, 128)]
 CHUNK_DZ = [[0], [1, 7], [2, 6], [3, 5], [4]]
 OWN = [0, 16, 48, 80, 112]
-RING = [(3, 0), (5, 1)] + [(dz, xr) for dz in (1, 2, 6, 7) for xr in range(2)]
+RING = [(3, 0), (5, 1), (2, 1), (6, 0), (2, 0), (6, 1), (1, 1), (7, 0), (1, 0), (7, 1)]
 CA = 512
 CB = FB - CA
 PA, PB = pl.ds(0, CA), pl.ds(CA, CB)
@@ -94,28 +94,25 @@
     def ag_begin(buf, i):
         own = buf.at[pl.ds(0, 32)]
         send(own, buf.at[pl.ds(POS[7], 32)], ag_s.at[i], ag_r.at[i, 1], zdev(1))
-        send(own, buf.at[pl.ds(POS[1], 32)], ag_s.at[i], ag_r.at[i, 2], zdev(-1))
+        send(own, buf.at[pl.ds(POS[1], 32)], ag_s.at[i], ag_r.at[i, 1], zdev(-1))
         send(own, buf.at[pl.ds(32, 32)], ag_s.at[i], ag_r.at[i, 0], xdev)
         send(own, buf.at[pl.ds(64, 32)], ag_s.at[i], sib_r.at[i, 0], sib)
 
     def ag_cross(buf, i):
         got = buf.at[pl.ds(32, 32)]
         await_bytes(got, ag_r.at[i, 0])
-        send(got, buf.at[pl.ds(POS[7] + 32, 32)], ag_s.at[i], ag_r.at[i, 3], zdev(1))
-        send(got, buf.at[pl.ds(POS[1] + 32, 32)], ag_s.at[i], ag_r.at[i, 4], zdev(-1))
+        send(got, buf.at[pl.ds(POS[7] + 32, 32)], ag_s.at[i], ag_r.at[i, 2], zdev(1))
+        send(got, buf.at[pl.ds(POS[1] + 32, 32)], ag_s.at[i], ag_r.at[i, 2], zdev(-1))
         send(got, buf.at[pl.ds(96, 32)], ag_s.at[i], sib_r.at[i, 0], sib)
 
     def ag_step(buf, i, j):
-        for xr in range(2):
+        for xr in range(2 if j < 4 else 1):
+            await_bytes(buf.at[pl.ds(POS[j], 64)], ag_r.at[i, 2 * j - 1 + xr])
             for way, (dz, ahead, nz) in enumerate(((NZ - j, 1, NZ - j - 1), (j, -1, j + 1))):
-                if j == 4 and way != xr:
-                    continue
-                piece = buf.at[pl.ds(POS[dz] + 32 * xr, 32)]
-                await_bytes(piece, ag_r.at[i, 4 * (j - 1) + 1 + 2 * xr + way])
                 if j < 3 or (j == 3 and way == xr):
                     send(
-                        piece, buf.at[pl.ds(POS[nz] + 32 * xr, 32)], ag_s.at[i],
-                        ag_r.at[i, 4 * j + 1 + 2 * xr + way], zdev(ahead),
+                        buf.at[pl.ds(POS[dz] + 32 * xr, 32)], buf.at[pl.ds(POS[nz] + 32 * xr, 32)], ag_s.at[i],
+                        ag_r.at[i, 2 * j + 1 + xr if j < 3 else 7], zdev(ahead),
                     )
         for dz in CHUNK_DZ[j]:
             send(buf.at[pl.ds(POS[dz], 64)], buf.at[pl.ds(POS[dz] + 64, 64)], ag_s.at[i], sib_r.at[i, j], sib)
@@ -239,7 +236,6 @@
         rows = pl.ds(64 * dz + 32 * xr, 32)
         total = part[pl.ds(POS[dz] + 32 * xr, 32)].astype(F32) + sb[rows].astype(F32)
         if (dz, xr) in RING:
-            await_bytes(rr.at[rows], sc_ring.at[i, RING.index((dz, xr))])
             total = total + rr[rows].astype(F32)
         q[rows] = total.astype(BF16)
         way = 1 if dz < 4 or (dz == 4 and xr == 0) else -1
@@ -249,11 +245,13 @@
             send(q.at[rows], fin.at[slot], sc_s.at[i], sc_fin.at[i], dev)
         else:
             to = 64 * (dz - way) + 32 * xr
-            send(q.at[rows], rr.at[pl.ds(to, 32)], sc_s.at[i], sc_ring.at[i, RING.index((dz - way, xr))], zdev(way))
+            send(q.at[rows], rr.at[pl.ds(to, 32)], sc_s.at[i], sc_ring.at[i, RING.index((dz - way, xr)) // 2], zdev(way))
 
     def sc_chunk(part, sb, q, rr, fin, i, chunk, late):
         if not late:
             await_bytes(sb.at[pl.ds(0, CHUNKS[chunk][1] // 2)], sc_sib.at[i, chunk])
+        if (chunk, 1 - late) in RING:
+            await_bytes(rr.at[pl.ds(0, 64)], sc_ring.at[i, RING.index((chunk, 1 - late)) // 2])
         for dz, xr in ((chunk, 1 - late), (NZ - chunk, late)):
             sc_piece(part, sb, q, rr, fin, i, dz, xr)
 
@@ -285,8 +283,8 @@
         return carry
 
     lax.fori_loop(0, 8, conv_tile, 0)
+    ag_begin(mx, 1)
     ag_cross(ct, 0)
-    ag_begin(mx, 1)
     load_wo.wait()
     def cot_chunk(c):
         if c > 0:
@@ -310,12 +308,9 @@
         if c < 4:
             cot_chunk(c + 1)
         mixed_chunk(c)
+        rs_second(gp, 0, c)
         if c > 0:
-            rs_second(gp, 0, c - 1)
             rs_second(hp, 1, c - 1)
-        if c > 1:
-            rs_final(c - 2)
-    rs_second(gp, 0, 4)
     rs_second(hp, 1, 4)
 
     def mgrad_part(c):
@@ -388,9 +383,9 @@
             for n in range(8):
                 kgrad_ref[:, 128 * n : 128 * (n + 1)] = (kg[n, 0:9] + kg[NZ + n, 0:9]) * FACTOR
 
-    at_first(hv, 0, 0)
-    at_first(hv, 0, 1)
-    at_first(hv, 0, 2)
+    for c in range(3):
+        rs_final(c)
+        at_first(hv, 0, c)
     rs_final(3)
     rs_final(4)
     at_first(hv, 0, 4)
@@ -420,11 +415,11 @@
     mgrad_part(1)
     mgrad_sum(2, 1)
     result_part(4)
+    mgrad_sum(1, 0)
     at_second(av, 1, 1)
-    mgrad_sum(1, 0)
     result_sum(4, 0)
+    mgrad_sum(1, 1)
     at_second(av, 1, 0)
-    mgrad_sum(1, 1)
     result_part(3)
     result_sum(3, 0)
     grad_in(0, 2)
@@ -442,10 +437,10 @@
     grad_in(4, 6)
     k_stage(2)
     result_sum(1, 0)
-    k_stage(4)
     result_sum(1, 1)
     grad_in(6, 8)
     grad_out(0, 7)
+    k_stage(4)
     k_stage(3)
     result_ref[...] = sc_total(pr, sbr, finr, 1)
 
@@ -491,9 +486,9 @@
         pltpu.VMEM((3, COLS, DB), BF16), pltpu.VMEM((COLS, DB), F32), pltpu.VMEM((2, COLS, DB), F32),
         pltpu.VMEM((8, 16, 128), F32), pltpu.VMEM((8, 16, 128), F32), pltpu.VMEM((7, 16, 128), F32),
         pltpu.VMEM((16, 128), F32), pltpu.VMEM((16, 16, 128), F32),
-        dma((5,)), dma, dma, dma((2,)), dma((2, 17)), dma((2, 5)),
+        dma((5,)), dma, dma, dma((2,)), dma((2, 8)), dma((2, 5)),
         dma((2,)), dma((3, 5)), dma((2,)), dma((2, 5, 2)),
-        dma((2,)), dma((2, 5)), dma((2, len(RING))), dma((2,)), dma, dma, dma((3,)), dma((3,)),
+        dma((2,)), dma((2, 5)), dma((2, len(RING) // 2)), dma((2,)), dma, dma, dma((3,)), dma((3,)),
     ]
     held = pl.pallas_call(
         kernel,

time: 101 us -> 100 us (0.990)
  no operation moved by 1% of the time
where the time goes in v5:
time: 100 us
  Pallas kernels  99.5 us (100%)
    pallas_call x1, Pallas kernels, on_device(): pl.pallas_call(kernel, out_shape=[pltpu.VMEM(*x) for x in shapes], in_spe...  96.3 us
    pallas_call x1, Pallas kernels, on_device(): pl.pallas_call(write_out, out_shape=[jax.ShapeDtypeStruct(*x) for x in sh...  3.2 us

profile of v5, /device:TPU:1, one launch (start us, length us, event | category | flops | bytes accessed | tf_op | source)
XLA Modules:
  0.0 100.3 jit_solution(4387714403299224416)
XLA Ops:
  0.6 96.3 %block.1 = (f32[32,1024]{1,0:T(8,128)S(1)}, f32[32,1024]{1,0:T(8,128)S(1)}, f32[9,1024]{1,0:T(8,128)S(1)}, f32[1024,896]{1,0:T(8,128)S(1)}, f32[896,1024]{1,0:T(8,128)S(1)}) custom-call(bf16[32,1024]{1,0:T(8,128)(2,1)} %bitcast.6, bf16[32,1024]{1,0:T(8,128)(2,1)} %bitcast.7, f32[9,1024]{1,0:T(8,128)} %taps_hbm.1, bf16[1024,896]{1,0:T(8,128)(2,1)} %wi_hbm.1, ...), custom_call_target="tpu_custom_call" | custom-call | flops 11274289152 | bytes 12582912 | tf_op jit(solution)/shard_map/block/pallas_call | solution.py:493
  97.0 3.2 %write_out.1 = (f32[32,1024]{1,0:T(8,128)}, f32[32,1024]{1,0:T(8,128)}, f32[9,1024]{1,0:T(8,128)}, f32[1024,896]{1,0:T(8,128)}, f32[896,1024]{1,0:T(8,128)}) custom-call(f32[32,1024]{1,0:T(8,128)S(1)} %get-tuple-element.15.refs_0_, f32[32,1024]{1,0:T(8,128)S(1)} %get-tuple-element.16.refs_1_, f32[9,1024]{1,0:T(8,128)S(1)} %get-tuple-element.17.refs_2_, ...), custom_call_target="tpu_custom_call" | custom-call | tf_op jit(solution)/shard_map/write_out/pallas_call | solution.py:505
